TPU v7x, 32 devices: a whole 2x2x4 slice. The times are simulated.
32 devices in a mesh: dp: 8 (over z, x), mp: 4 (over y, core).
Axes of the slice: x: 2, y: 2, z: 4, core: 2. Of those that a mesh axis runs over, the one named last changes fastest.
Arguments:
- row_ids: int32 [8192, 8, 16], P('dp'), may hold values from 0 to 262143, as said below
- bag_counts: int32 [8192, 8], P('dp'), may hold values from 1 to 16
- labels: int32 [8192, 5], P('dp'), may hold values from 0 to 1
- label_mask: int32 [8192, 5], P('dp'), may hold values from 0 to 1, as said below
- tables: float32 [8, 262144, 64], P(None, ('dp', 'mp')), may hold values from -6 to 6
- table_mom: float32 [8, 262144, 64], P(None, ('dp', 'mp')), may hold values from -5.722046e-06 to 5.722046e-06
- table_avg: float32 [8, 262144, 64], P(None, ('dp', 'mp')), may hold values from -6 to 6
- w_in: float32 [8, 512, 1024], P(None, 'dp', 'mp'), may hold values from -1.75 to 1.75
- w_in_mom: float32 [8, 512, 1024], P(None, 'dp', 'mp'), may hold values from -0.00024414062 to 0.00024414062
- w_in_avg: float32 [8, 512, 1024], P(None, 'dp', 'mp'), may hold values from -1.75 to 1.75
- w_out: float32 [8, 1024, 512], P(None, 'mp', 'dp'), may hold values from -1 to 1
- w_out_mom: float32 [8, 1024, 512], P(None, 'mp', 'dp'), may hold values from -0.00048828125 to 0.00048828125
- w_out_avg: float32 [8, 1024, 512], P(None, 'mp', 'dp'), may hold values from -1 to 1
- gate_w: float32 [5, 512, 8], replicated, may hold values from -0.75 to 0.75
- gate_mom: float32 [5, 512, 8], replicated, may hold values from -0.0024414062 to 0.0024414062
- gate_avg: float32 [5, 512, 8], replicated, may hold values from -0.75 to 0.75
- tower_w: float32 [5, 512, 128], replicated, may hold values from -1 to 1
- tower_w_mom: float32 [5, 512, 128], replicated, may hold values from -0.0048828125 to 0.0048828125
- tower_w_avg: float32 [5, 512, 128], replicated, may hold values from -1 to 1
- tower_v: float32 [5, 128], replicated, may hold values from -2.5 to 2.5
- tower_v_mom: float32 [5, 128], replicated, may hold values from -0.0234375 to 0.0234375
- tower_v_avg: float32 [5, 128], replicated, may hold values from -2.5 to 2.5
Outputs:
- loss_sum: float32 [], replicated
- tables_new: float32 [8, 262144, 64], P(None, ('dp', 'mp'))
- table_mom_new: float32 [8, 262144, 64], P(None, ('dp', 'mp'))
- table_avg_new: float32 [8, 262144, 64], P(None, ('dp', 'mp'))
- w_in_new: float32 [8, 512, 1024], P(None, 'dp', 'mp')
- w_in_mom_new: float32 [8, 512, 1024], P(None, 'dp', 'mp')
- w_in_avg_new: float32 [8, 512, 1024], P(None, 'dp', 'mp')
- w_out_new: float32 [8, 1024, 512], P(None, 'mp', 'dp')
- w_out_mom_new: float32 [8, 1024, 512], P(None, 'mp', 'dp')
- w_out_avg_new: float32 [8, 1024, 512], P(None, 'mp', 'dp')
- gate_new: float32 [5, 512, 8], replicated
- gate_mom_new: float32 [5, 512, 8], replicated
- gate_avg_new: float32 [5, 512, 8], replicated
- tower_w_new: float32 [5, 512, 128], replicated
- tower_w_mom_new: float32 [5, 512, 128], replicated
- tower_w_avg_new: float32 [5, 512, 128], replicated
- tower_v_new: float32 [5, 128], replicated
- tower_v_mom_new: float32 [5, 128], replicated
- tower_v_avg_new: float32 [5, 128], replicated
Inputs may be any that keep to these rules, and one draw needn't show every extreme that they name: `row_ids`: the samples split into aligned blocks of 256 (those of one device). In each block, over all 8 x 16 slots, live or not, the rows named lie on each owner (row id // 8192) at most 2048 times, and one owner, the same for all blocks of a draw, is named exactly 2048 times in every block. `label_mask`: the share of ones rises from about a quarter at the first sample to about three quarters at the last.
All inputs are finite; a program needn't handle non-finite values.
Results may differ from a plain program's by a relative error of at most 0.03.
Values may be sent and summed in bfloat16 or wider, within the bound.
No kernel may reach another device: no remote copies, remote signals or barrier semaphores. Data moves between devices by JAX's collectives and lax.ppermute only.
A program may use at most 320 MiB of HBM per device.

v0:
```python
import jax
import jax.numpy as jnp
from jax import lax
from jax.sharding import PartitionSpec as P

highest = lax.Precision.HIGHEST
mu_rate = 0.5
avg_decay = 0.5
task_weights = (1.0, 0.6, 0.8, 0.4, 1.2)
rates = (5000000.0, 12000.0, 3500.0, 1000.0, 370.0, 200.0)
slot_block = 128


def gelu_grad(values_in):
    result, pullback = jax.vjp(jax.nn.gelu, values_in)
    return (result, pullback(jnp.ones_like(values_in))[0])


def nesterov(weight, moment, average, grad, rate):
    moment_new = mu_rate * moment + grad
    weight_new = weight - rate * (grad + mu_rate * moment_new)
    average_new = avg_decay * average + (1.0 - avg_decay) * weight_new
    return (weight_new, moment_new, average_new)


def bucket_places(target, owner_total):
    slot_total = target.shape[0]
    block_count = slot_total // slot_block
    one_hot = (target[:, None] == jnp.arange(owner_total, dtype=jnp.int32)[None, :]).astype(
        jnp.bfloat16
    )
    blocked = one_hot.reshape(block_count, slot_block, owner_total)
    lower = (jnp.arange(slot_block)[:, None] > jnp.arange(slot_block)[None, :]).astype(jnp.bfloat16)
    within = jnp.einsum("ij,bjo->bio", lower, blocked, preferred_element_type=jnp.float32)
    block_sums = jnp.sum(blocked.astype(jnp.float32), axis=1)
    before = jnp.cumsum(block_sums, axis=0) - block_sums
    counted = (within + before[:, None, :]).reshape(slot_total, owner_total)
    place = jnp.sum(counted * one_hot.astype(jnp.float32), axis=1)
    return place.astype(jnp.int32)


def head_backward(
    x_rows, y_rows, label_rows, mask_rows, gate_low, tower_low, tower_v, sample_total
):
    gate_logits = jnp.einsum("rf,kfe->rke", x_rows, gate_low, preferred_element_type=jnp.float32)
    gate_probs = jax.nn.softmax(gate_logits, axis=-1)
    mixture = jnp.einsum("rke,ref->rkf", gate_probs, y_rows, precision=highest).astype(jnp.bfloat16)
    tower_pre = jnp.einsum("rkf,kfc->rkc", mixture, tower_low, preferred_element_type=jnp.float32)
    tower_act, slopes = gelu_grad(tower_pre)
    logits = jnp.einsum("rkc,kc->rk", tower_act, tower_v, precision=highest)
    label_f = label_rows.astype(jnp.float32)
    weighting = jnp.asarray(task_weights, jnp.float32) * mask_rows.astype(jnp.float32)
    loss_part = jnp.sum(weighting * (jax.nn.softplus(logits) - label_f * logits))
    d_logits = weighting * (jax.nn.sigmoid(logits) - label_f) / sample_total
    d_tower_v = jnp.einsum("rk,rkc->kc", d_logits, tower_act, precision=highest)
    d_pre = (d_logits[:, :, None] * tower_v[None] * slopes).astype(jnp.bfloat16)
    d_tower_w = jnp.einsum("rkf,rkc->kfc", mixture, d_pre, preferred_element_type=jnp.float32)
    d_mixture = jnp.einsum("rkc,kfc->rkf", d_pre, tower_low, preferred_element_type=jnp.float32)
    d_probs = jnp.einsum("rkf,ref->rke", d_mixture, y_rows, precision=highest)
    d_logit_gate = (
        gate_probs * (d_probs - jnp.sum(gate_probs * d_probs, axis=-1, keepdims=True))
    ).astype(jnp.bfloat16)
    d_expert = jnp.einsum("rke,rkf->ref", gate_probs, d_mixture, precision=highest).astype(
        jnp.bfloat16
    )
    d_gate_w = jnp.einsum("rf,rke->kfe", x_rows, d_logit_gate, preferred_element_type=jnp.float32)
    d_x_gate = jnp.einsum("rke,kfe->rf", d_logit_gate, gate_low, preferred_element_type=jnp.float32)
    return (loss_part, d_gate_w, d_tower_w, d_tower_v, d_x_gate, d_expert)


def expert_fold(block_rows, activated, slopes, w_out_full):
    d_w_out = jnp.einsum("beh,bef->ehf", activated, block_rows, preferred_element_type=jnp.float32)
    d_act = jnp.einsum("bef,ehf->beh", block_rows, w_out_full, preferred_element_type=jnp.float32)
    d_rows = (d_act * slopes).astype(jnp.bfloat16)
    return (d_w_out, d_rows)


def body(
    row_ids,
    bag_counts,
    labels,
    label_mask,
    tables,
    table_mom,
    table_avg,
    w_in,
    w_in_mom,
    w_in_avg,
    w_out,
    w_out_mom,
    w_out_avg,
    gate_w,
    gate_mom,
    gate_avg,
    tower_w,
    tower_w_mom,
    tower_w_avg,
    tower_v,
    tower_v_mom,
    tower_v_avg,
):
    n_model = lax.axis_size("mp")
    n_data = lax.axis_size("dp")
    owner_total = lax.axis_size(("dp", "mp"))
    mp_rank = lax.axis_index("mp")
    per_group, table_count, bag_size = row_ids.shape
    per_device = per_group // n_model
    rows_own = tables.shape[1]
    emb_width = tables.shape[2]
    sample_total = float(per_group * n_data)
    own_ids = lax.dynamic_slice_in_dim(row_ids, mp_rank * per_device, per_device, 0).reshape(-1)
    own_counts = lax.dynamic_slice_in_dim(bag_counts, mp_rank * per_device, per_device, 0)
    slot_total = own_ids.shape[0]
    capacity = 2 * slot_total // owner_total
    target = own_ids // rows_own
    table_of = jnp.arange(slot_total, dtype=jnp.int32) // bag_size % table_count
    local_row = table_of * rows_own + own_ids % rows_own
    position = bucket_places(target, owner_total)
    bucket = target * capacity + position
    filler = (
        jnp.full((owner_total * capacity,), -1, jnp.int32)
        .at[bucket]
        .set(jnp.arange(slot_total, dtype=jnp.int32))
    )
    filled = filler >= 0
    source = jnp.maximum(filler, 0)
    requests = jnp.where(filled, local_row[source], 0).reshape(owner_total, capacity)
    asked_rows = lax.all_to_all(requests, ("dp", "mp"), split_axis=0, concat_axis=0, tiled=True)
    table_flat = tables.reshape(table_count * rows_own, emb_width)
    found_rows = table_flat[asked_rows].astype(jnp.bfloat16)
    answered = lax.all_to_all(
        found_rows, ("dp", "mp"), split_axis=0, concat_axis=0, tiled=True
    ).reshape(owner_total * capacity, emb_width)
    slot_rows = (
        answered[bucket].astype(jnp.float32).reshape(per_device, table_count, bag_size, emb_width)
    )
    slot_share = (jnp.arange(bag_size)[None, None, :] < own_counts[:, :, None]).astype(
        jnp.float32
    ) / own_counts[:, :, None].astype(jnp.float32)
    pooled = jnp.sum(slot_rows * slot_share[..., None], axis=2).reshape(
        per_device, table_count * emb_width
    )
    x_sub = pooled.astype(jnp.bfloat16)
    x_all = lax.all_gather(x_sub, "mp", axis=0, tiled=True)
    w_in_full, w_out_full = (
        lax.all_gather(w_in.astype(jnp.bfloat16), "dp", axis=1, tiled=True),
        lax.all_gather(w_out.astype(jnp.bfloat16), "dp", axis=2, tiled=True),
    )
    gate_low = gate_w.astype(jnp.bfloat16)
    tower_low = tower_w.astype(jnp.bfloat16)
    label_rows = lax.dynamic_slice_in_dim(labels, mp_rank * per_device, per_device, 0)
    mask_rows = lax.dynamic_slice_in_dim(label_mask, mp_rank * per_device, per_device, 0)
    hidden = jnp.einsum("bf,efh->beh", x_all, w_in_full, preferred_element_type=jnp.float32)
    act_f, slopes = gelu_grad(hidden)
    activated = act_f.astype(jnp.bfloat16)
    y_rows = lax.psum_scatter(
        jnp.einsum(
            "beh,ehf->bef", activated, w_out_full, preferred_element_type=jnp.float32
        ).astype(jnp.bfloat16),
        "mp",
        scatter_dimension=0,
        tiled=True,
    ).astype(jnp.float32)
    loss_part, d_gate_w, d_tower_w, d_tower_v, d_x_gate, d_expert = head_backward(
        x_sub, y_rows, label_rows, mask_rows, gate_low, tower_low, tower_v, sample_total
    )
    loss_sum, d_gate_w, d_tower_w, d_tower_v = lax.psum(
        (loss_part, d_gate_w, d_tower_w, d_tower_v), ("dp", "mp")
    )
    d_w_out, d_hidden = expert_fold(
        lax.all_gather(d_expert, "mp", axis=0, tiled=True), activated, slopes, w_out_full
    )
    d_features = (
        lax.psum_scatter(
            jnp.einsum(
                "beh,efh->bf", d_hidden, w_in_full, preferred_element_type=jnp.float32
            ).astype(jnp.bfloat16),
            "mp",
            scatter_dimension=0,
            tiled=True,
        ).astype(jnp.float32)
        + d_x_gate
    )
    d_w_in = jnp.einsum("bf,beh->efh", x_all, d_hidden, preferred_element_type=jnp.float32)
    d_w_in_own, d_w_out_own = (
        lax.psum_scatter(d_w_in.astype(jnp.bfloat16), "dp", scatter_dimension=1, tiled=True).astype(
            jnp.float32
        ),
        lax.psum_scatter(
            d_w_out.astype(jnp.bfloat16), "dp", scatter_dimension=2, tiled=True
        ).astype(jnp.float32),
    )
    slot_grads = (
        d_features.reshape(per_device, table_count, 1, emb_width) * slot_share[..., None]
    ).reshape(slot_total, emb_width)
    outgoing = jnp.where(filled[:, None], slot_grads[source], 0.0).reshape(
        owner_total, capacity, emb_width
    )
    returned = lax.all_to_all(
        outgoing.astype(jnp.bfloat16), ("dp", "mp"), split_axis=0, concat_axis=0, tiled=True
    ).astype(outgoing.dtype)
    d_tables = (
        jnp.zeros((table_count * rows_own, emb_width), jnp.float32)
        .at[asked_rows.reshape(-1)]
        .add(returned.reshape(-1, emb_width))
        .reshape(tables.shape)
    )
    table_new = nesterov(tables, table_mom, table_avg, d_tables, rates[0])
    w_in_new = nesterov(w_in, w_in_mom, w_in_avg, d_w_in_own, rates[1])
    w_out_new = nesterov(w_out, w_out_mom, w_out_avg, d_w_out_own, rates[2])
    gate_new = nesterov(gate_w, gate_mom, gate_avg, d_gate_w, rates[3])
    tower_new = nesterov(tower_w, tower_w_mom, tower_w_avg, d_tower_w, rates[4])
    vector_new = nesterov(tower_v, tower_v_mom, tower_v_avg, d_tower_v, rates[5])
    return (
        loss_sum,
        table_new[0],
        table_new[1],
        table_new[2],
        w_in_new[0],
        w_in_new[1],
        w_in_new[2],
        w_out_new[0],
        w_out_new[1],
        w_out_new[2],
        gate_new[0],
        gate_new[1],
        gate_new[2],
        tower_new[0],
        tower_new[1],
        tower_new[2],
        vector_new[0],
        vector_new[1],
        vector_new[2],
    )


def solution(mesh):
    placed = (
        P("dp", None, None),
        P("dp", None),
        P("dp", None),
        P("dp", None),
        P(None, ("dp", "mp"), None),
        P(None, ("dp", "mp"), None),
        P(None, ("dp", "mp"), None),
        P(None, "dp", "mp"),
        P(None, "dp", "mp"),
        P(None, "dp", "mp"),
        P(None, "mp", "dp"),
        P(None, "mp", "dp"),
        P(None, "mp", "dp"),
        P(),
        P(),
        P(),
        P(),
        P(),
        P(),
        P(),
        P(),
        P(),
    )
    return jax.shard_map(
        body,
        mesh=mesh,
        in_specs=placed,
        out_specs=(
            P(),
            P(None, ("dp", "mp"), None),
            P(None, ("dp", "mp"), None),
            P(None, ("dp", "mp"), None),
            P(None, "dp", "mp"),
            P(None, "dp", "mp"),
            P(None, "dp", "mp"),
            P(None, "mp", "dp"),
            P(None, "mp", "dp"),
            P(None, "mp", "dp"),
            P(),
            P(),
            P(),
            P(),
            P(),
            P(),
            P(),
            P(),
            P(),
        ),
        check_vma=False,
    )
```

profile of v0, /device:TPU:0, one launch (start us, length us, event | category | flops | bytes accessed | tf_op | source)
XLA Modules:
  0.0 2484.9 jit_solution(14200065218994291126)
XLA Ops:
  13.4 120.1 %scatter_custom_fusion = s32[65536]{0:T(1024)S(1)} fusion(s32[32768]{0:T(1024)S(1)} %bitcast.163, s32[32768]{0:T(1024)S(1)} %iota.36, s32[]{:T(128)} %constant.47.clone.1), kind=kCustom, calls=%fused_computation.127 | custom fusion | bytes 262148 | tf_op jit(solution)/shard_map/scatter | solution.py:123
  133.6 362.7 %gather_fusion = s32[65536]{0:T(1024)S(1)} fusion(s32[32768]{0:T(1024)S(1)} %fusion.54, s32[65536]{0:T(1024)S(1)} %maximum_clamp_fusion), kind=kCustom, calls=%fused_computation | custom fusion | bytes 786432 | tf_op jit(solution)/shard_map/gather | solution.py:127
  504.4 19.2 copy.232
  524.0 227.6 %gather_fusion.1 = bf16[65536,64]{1,0:T(8,128)(2,1)} fusion(bf16[65536,64]{1,0:T(8,128)(2,1)} %bitcast.149, s32[65536]{0:T(1024)S(1)} %broadcast_clamp_fusion), kind=kCustom, calls=%fused_computation.1 | custom fusion | bytes 17039360 | tf_op jit(solution)/shard_map/gather | solution.py:130
  751.6 15.8 copy.238
  776.1 206.3 %all-to-all-done.1 = bf16[32,2048,64]{1,2,0:T(8,128)(2,1)} async-done(((bf16[32,2048,64]{1,2,0:T(8,128)(2,1)}), bf16[32,2048,64]{1,2,0:T(8,128)(2,1)}, u32[]{:S(2)}, u32[]{:S(2)}) %all-to-all-start.1) | async-done | bytes 8388640 | tf_op jit(solution)/shard_map/all_to_all | solution.py:131
  982.4 15.5 copy.239
  998.0 118.4 %gather_fusion.2 = bf16[32768,64]{1,0:T(8,128)(2,1)} fusion(bf16[65536,64]{1,0:T(8,128)(2,1)} %bitcast.150, s32[32768]{0:T(1024)S(1)} %broadcast_clamp_fusion.1), kind=kCustom, calls=%fused_computation.2 | custom fusion | bytes 8519680 | tf_op jit(solution)/shard_map/gather | solution.py:135
  1126.1 21.1 all-gather.5.cloned.1.call-done
  1154.9 44.4 %all-gather.9.cloned.1.call-done = bf16[8,256,512]{1,2,0:T(8,128)(2,1)} async-done(((bf16[8,256,64]{1,2,0:T(8,128)(2,1)}), bf16[8,256,512]{1,2,0:T(8,128)(2,1)}) %all-gather.9.cloned.1.call-update) | async-done | bytes 2097168 | tf_op jit(solution)/shard_map/all_gather | solution.py:147
  1209.0 68.9 %reduce-scatter.5.cloned.1.call-done = bf16[256,8,512]{2,0,1:T(8,128)(2,1)} async-done(((bf16[1024,8,512]{2,0,1:T(8,128)(2,1)}), bf16[256,8,512]{2,0,1:T(8,128)(2,1)}) %reduce-scatter.5.cloned.1.call-update) | async-done | bytes 2097168 | tf_op jit(solution)/shard_map/reduce_scatter | solution.py:156
  1295.5 57.9 %all-gather.11.cloned.1.call-done = bf16[1024,8,512]{2,1,0:T(8,128)(2,1)} async-done(((bf16[256,8,512]{2,1,0:T(8,128)(2,1)}), bf16[1024,8,512]{2,1,0:T(8,128)(2,1)}) %all-gather.11.cloned.1.call-update) | async-done | bytes 8388624 | tf_op jit(solution)/shard_map/all_gather | solution.py:171
  1353.5 12.1 copy.269
  1365.6 11.4 fusion.13
  1417.3 224.4 %gather_fusion.3 = bf16[65536,64]{1,0:T(8,128)(2,1)} fusion(bf16[32768,64]{1,0:T(8,128)(2,1)} %bitcast_multiply_fusion, s32[65536]{0:T(1024)S(1)} %copy-done.14), kind=kCustom, calls=%fused_computation.3 | custom fusion | bytes 17039360 | tf_op jit(solution)/shard_map/gather | solution.py:196
  1641.7 15.9 copy.257
  1685.2 220.1 %all-reduce = (f32[]{:T(128)}, f32[5,128]{1,0:T(8,128)S(1)}) all-reduce(f32[]{:T(128)} %get-tuple-element.160, f32[5,128]{1,0:T(8,128)S(1)} %bitcast.168), channel_id=1, replica_groups=mesh['dp'=8,'mp'=4] {'dp','mp'}, use_global_device_ids=true, to_apply=%region_10.11 | all-reduce | flops 641 | bytes 5128 | tf_op jit(solution)/shard_map/psum | solution.py:167
  1919.4 17.9 copy.286
  1937.3 414.3 %scatter_custom_fusion.1 = f32[65536,64]{1,0:T(8,128)} fusion(s32[65536]{0:T(1024)} %bitcast.166, f32[65536,64]{1,0:T(8,128)} %bitcast.156, f32[]{:T(128)} %constant.57.clone.1), kind=kCustom, calls=%fused_computation.16 | custom fusion | flops 4194304 | bytes 16777728 | tf_op jit(solution)/shard_map/scatter-add | solution.py:205
  2351.6 26.2 %copy.287 = f32[8,8192,64]{1,0,2:T(8,128)} copy(f32[8,8192,64]{2,1,0:T(8,128)} %bitcast.151) | data formatting | bytes 33554432 | tf_op jit(solution)/shard_map/reshape | solution.py:206
  2377.8 50.4 %fusion.2 = (f32[8,8192,64]{1,0,2:T(8,128)}, f32[8,8192,64]{1,0,2:T(8,128)}, f32[8,8192,64]{1,0,2:T(8,128)}) fusion(f32[8,8192,64]{1,2,0:T(8,128)} %param.29, f32[8,8192,64]{1,0,2:T(8,128)} %copy.287, f32[8,8192,64]{1,2,0:T(8,128)} %param.28, f32[8,8192,64]{1,2,0:T(8,128)} %param.27), kind=kLoop, calls=%fused_computation.11 | loop fusion | flops 33554432 | bytes 117440512 | tf_op jit(solution)/shard_map/add | solution.py:22
  2428.3 19.6 copy.274
  2447.9 15.1 copy.272
  2463.0 15.1 copy.273
  (166 shorter events, 149.5 us)
Async XLA Ops:
  133.6 362.7 %copy-start.13 = (s32[65536]{0:T(1024)}, s32[65536]{0:T(1024)S(1)}, u32[]{:S(2)}) copy-start(s32[65536]{0:T(1024)S(1)} %maximum_clamp_fusion) | copy-start | bytes 786436
  497.1 26.6 %all-to-all-start = ((s32[32,1,2048]{2,1,0:T(1,128)}), s32[32,1,2048]{2,1,0:T(1,128)S(1)}, u32[]{:S(2)}, u32[]{:S(2)}) async-start(s32[32,1,2048]{2,1,0:T(1,128)} %bitcast.8), calls=%async_computation | async-start | bytes 524288 | tf_op jit(solution)/shard_map/all_to_all | solution.py:128
  523.7 228.0 %copy-start.11 = (s32[32,1,2048]{2,1,0:T(1,128)}, s32[32,1,2048]{2,1,0:T(1,128)S(1)}, u32[]{:S(2)}) copy-start(s32[32,1,2048]{2,1,0:T(1,128)S(1)} %all-to-all-done) | copy-start | bytes 786436
  767.4 215.0 %all-to-all-start.1 = ((bf16[32,2048,64]{1,2,0:T(8,128)(2,1)}), bf16[32,2048,64]{1,2,0:T(8,128)(2,1)}, u32[]{:S(2)}, u32[]{:S(2)}) async-start(bf16[32,2048,64]{1,2,0:T(8,128)(2,1)} %copy.238), calls=%async_computation.1 | async-start | bytes 16777216 | tf_op jit(solution)/shard_map/all_to_all | solution.py:131
  773.4 352.7 %all-gather.7.cloned.1.call-start = ((), (), s32[]{:S(2)}) async-start(), calls=%async_computation.8 | async-start | bytes 2359296 | tf_op jit(solution)/shard_map/all_gather | solution.py:146
  774.2 373.0 %all-gather.5.cloned.1.call-start = ((), (), s32[]{:S(2)}) async-start(), calls=%async_computation.7 | async-start | bytes 1310720 | tf_op jit(solution)/shard_map/all_gather | solution.py:144
  776.1 340.3 %copy-start.5 = (f32[256,8,16]{2,1,0:T(8,128)}, f32[256,8,16]{2,1,0:T(8,128)S(1)}, u32[]{:S(2)}) copy-start(f32[256,8,16]{2,1,0:T(8,128)S(1)} %convert_divide_fusion) | copy-start | bytes 393220
  1125.2 74.1 %all-gather.9.cloned.1.call-start = ((), (), s32[]{:S(2)}) async-start(), calls=%async_computation.9 | async-start | bytes 2359296 | tf_op jit(solution)/shard_map/all_gather | solution.py:147
  1126.0 151.8 %reduce-scatter.5.cloned.1.call-start = ((), (), s32[]{:S(2)}) async-start(), calls=%async_computation.10 | async-start | bytes 10485760 | tf_op jit(solution)/shard_map/reduce_scatter | solution.py:156
  1207.5 76.5 %copy-start.26 = (f32[5]{0:T(128)S(1)}, f32[5]{0:T(128)}, u32[]{:S(2)}) copy-start(f32[5]{0:T(128)} %constant.127.clone) | copy-start | bytes 64
  1207.5 146.0 %all-gather.11.cloned.1.call-start = ((), (), s32[]{:S(2)}) async-start(), calls=%async_computation.11 | async-start | bytes 10485760 | tf_op jit(solution)/shard_map/all_gather | solution.py:171
  1209.0 76.4 %copy-start.7 = (f32[256,5,8]{1,2,0:T(8,128)}, f32[256,5,8]{1,2,0:T(8,128)S(1)}, u32[]{:S(2)}) copy-start(f32[256,5,8]{1,2,0:T(8,128)S(1)} %copy.248) | copy-start | bytes 122884
  1295.0 114.4 %reduce-scatter.7.cloned.1.call-start = ((), (), s32[]{:S(2)}) async-start(), calls=%async_computation.12 | async-start | bytes 1310720 | tf_op jit(solution)/shard_map/reduce_scatter | solution.py:174
  1382.4 523.6 %all-reduce.4.cloned.1.call-start = ((), (), s32[]{:S(2)}) async-start(), calls=%async_computation.15 | async-start | bytes 2785280 | tf_op jit(solution)/shard_map/psum | solution.py:167
  1397.6 514.4 %reduce-scatter.9.cloned.1.call-start = ((), (), s32[]{:S(2)}) async-start(), calls=%async_computation.13 | async-start | bytes 2359296 | tf_op jit(solution)/shard_map/reduce_scatter | solution.py:186
  1667.6 251.7 %all-to-all-start.2 = ((bf16[32,2048,64]{1,2,0:T(8,128)(2,1)}), bf16[32,2048,64]{1,2,0:T(8,128)(2,1)}, u32[]{:S(2)}, u32[]{:S(2)}) async-start(bf16[32,2048,64]{1,2,0:T(8,128)(2,1)} %select_convert_fusion), calls=%async_computation.4 | async-start | bytes 16777216 | tf_op jit(solution)/shard_map/all_to_all | solution.py:199
  1672.4 232.9 %copy-start.24 = (f32[5,128]{1,0:T(8,128)S(1)}, f32[5,128]{1,0:T(8,128)}, u32[]{:S(2)}) copy-start(f32[5,128]{1,0:T(8,128)} %param.44) | copy-start | bytes 7684
  1672.4 232.9 %copy-start.25 = (f32[5,128]{1,0:T(8,128)S(1)}, f32[5,128]{1,0:T(8,128)}, u32[]{:S(2)}) copy-start(f32[5,128]{1,0:T(8,128)} %param.43) | copy-start | bytes 7684
  1672.4 235.2 %copy-start.4 = (f32[5,512,128]{2,1,0:T(8,128)S(1)}, f32[5,512,128]{2,1,0:T(8,128)}, u32[]{:S(2)}) copy-start(f32[5,512,128]{2,1,0:T(8,128)} %param.39) | copy-start | bytes 3932164
  1672.4 244.4 %reduce-scatter.11.cloned.1.call-start = ((), (), s32[]{:S(2)}) async-start(), calls=%async_computation.14 | async-start | bytes 2359296 | tf_op jit(solution)/shard_map/reduce_scatter | solution.py:189
  1683.6 228.4 %copy-start.16 = (f32[8,64,256]{2,1,0:T(8,128)S(1)}, f32[8,64,256]{2,1,0:T(8,128)}, u32[]{:S(2)}) copy-start(f32[8,64,256]{2,1,0:T(8,128)} %param.30) | copy-start | bytes 1572868
  1683.6 228.4 %copy-start.19 = (f32[8,64,256]{2,1,0:T(8,128)S(1)}, f32[8,64,256]{2,1,0:T(8,128)}, u32[]{:S(2)}) copy-start(f32[8,64,256]{2,1,0:T(8,128)} %param.32) | copy-start | bytes 1572868
  1685.2 226.8 %copy-start.20 = (f32[8,64,256]{2,1,0:T(8,128)S(1)}, f32[8,64,256]{2,1,0:T(8,128)}, u32[]{:S(2)}) copy-start(f32[8,64,256]{2,1,0:T(8,128)} %param.31) | copy-start | bytes 1572868
  1685.2 231.6 %copy-start.18 = (f32[8,256,64]{1,2,0:T(8,128)S(1)}, f32[8,256,64]{1,2,0:T(8,128)}, u32[]{:S(2)}) copy-start(f32[8,256,64]{1,2,0:T(8,128)} %param.33) | copy-start | bytes 1572868
  (21 other events, 377.6 us)
Sparse Core Ops, SparseCore 0:
  777.0 103.1 all-gather.6
  1125.3 21.8 all-gather.4
  1150.0 49.2 all-gather.8
  1207.6 70.1 reduce-scatter.4
  1295.1 58.2 all-gather.10
  1382.5 24.8 reduce-scatter.6
  1413.5 131.4 all-reduce.3
  1548.5 67.2 reduce-scatter.8
  1683.7 124.6 reduce-scatter.10
where the time goes:
time: 2500 us; the launch traced here: 2480 us
  local copies, waits for them, and re-layouts  1240 us (50%)
  other arithmetic  508 us (20%)
  waiting for transfers between devices  399 us (16%)
  blocking collectives  220 us (9%)
  matrix products  80.2 us (3%)
    scatter-add x1, other arithmetic, body(): d_tables = jnp.zeros((table_count * rows_own, emb_width), jnp.float32).at...  414 us
    gather x1, local copies, waits for them, and re-layouts, body(): local_row[source]  363 us
    gather x2, local copies, waits for them, and re-layouts, body(): slot_grads[source]  240 us
    gather x1, local copies, waits for them, and re-layouts, body(): found_rows = table_flat[asked_rows].astype(jnp.bfloat16)  228 us
    psum x1, blocking collectives, body(): lax.psum((loss_part, d_gate_w, d_tower_w, d_tower_v), ('dp', 'mp'))  220 us
    all_to_all x1, waiting for transfers between devices, body(): lax.all_to_all(found_rows, ('dp', 'mp'), split_axis=0, concat_axis=0, til...  206 us
    scatter x1, local copies, waits for them, and re-layouts, body(): filler = jnp.full((owner_total * capacity,), -1, jnp.int32).at[bucket].se...  120 us
    gather x1, local copies, waits for them, and re-layouts, body(): answered[bucket].astype(jnp.float32)  118 us
  transfers between devices with their start and end apart: 12, of which 5 were waited for; matrix products, arithmetic and copies ran while one was open for 19% of the time, Pallas kernels for 0%

commit v1 on v0

v1 whole, which is shorter than its diff:
```python
import functools
import math

import jax
import jax.numpy as jnp
from jax import lax
from jax.experimental import pallas as pl
from jax.experimental.pallas import tpu as pltpu
from jax.sharding import PartitionSpec as P

highest = lax.Precision.HIGHEST
mu_rate = 0.5
avg_decay = 0.5
task_weights = (1.0, 0.6, 0.8, 0.4, 1.2)
rates = (5000000.0, 12000.0, 3500.0, 1000.0, 370.0, 200.0)
both = ("dp", "mp")
lanes = 128
group = 16
flag_bit = 20
f32, bf16, i32 = jnp.float32, jnp.bfloat16, jnp.int32
vmem_limit = 58 * 2**20


def bits_of(size):
    return int(size).bit_length() - 1


def params(limit=vmem_limit):
    return pltpu.CompilerParams(vmem_limit_bytes=limit)


def gelu_pair(h):
    scale = math.sqrt(2.0 / math.pi)
    square = h * h
    t = jnp.tanh(scale * h * (1.0 + 0.044715 * square))
    half = 0.5 * (1.0 + t)
    slope = half + 0.5 * h * (1.0 - t * t) * scale * (1.0 + 3.0 * 0.044715 * square)
    return h * half, slope


def gelu_grad(values_in):
    result, pullback = jax.vjp(jax.nn.gelu, values_in)
    return (result, pullback(jnp.ones_like(values_in))[0])


def nesterov(weight, moment, average, grad, rate):
    moment_new = mu_rate * moment + grad
    weight_new = weight - rate * (grad + mu_rate * moment_new)
    average_new = avg_decay * average + (1.0 - avg_decay) * weight_new
    return (weight_new, moment_new, average_new)


class Ring:
    def __init__(self, n_data, n_model):
        self.n_model = n_model
        self.sizes = (2, n_model // 2, 2, n_data // 2)
        self.steps = (("mp", 1), ("mp", 2), ("dp", 1), ("dp", 2))
        self.axis_sizes = {"dp": n_data, "mp": n_model}

    def offset_of(self, place):
        total = 0
        rest = place
        for size, (axis, stride) in reversed(list(zip(self.sizes, self.steps))):
            digit = rest & (size - 1)
            rest = rest >> bits_of(size)
            weight = stride * (self.n_model if axis == "dp" else 1)
            total = total + digit * weight
        return total

    def swap(self, value, stage, distance):
        axis, stride = self.steps[stage]
        count = self.axis_sizes[axis]
        return lax.ppermute(value, axis, [(i, i ^ (distance * stride)) for i in range(count)])

    def reduce_scatter(self, value):
        for stage, size in enumerate(self.sizes):
            if size == 1:
                continue
            parts = value.reshape((size, -1) + value.shape[1:])
            total = parts[0].astype(f32)
            for distance in range(1, size):
                total = total + self.swap(parts[distance], stage, distance).astype(f32)
            value = total.astype(bf16) if stage < 3 else total
        return value[0]

    def all_gather(self, value):
        value = value[None]
        for stage in reversed(range(4)):
            size = self.sizes[stage]
            if size == 1:
                continue
            pieces = [value] + [self.swap(value, stage, d) for d in range(1, size)]
            value = jnp.concatenate(pieces, axis=0)
        return value


def bucket_kernel(pairs, cap_rows, starts, keys, out):
    owners = out.shape[0]
    lane = lax.broadcasted_iota(i32, (1, lanes), 1)
    body_rows = -(-(cap_rows + 1) // 8) * 8

    def one(o, carry):
        off = starts[o * pairs]
        row = lax.shift_right_logical(off, 7)
        shift = off & (lanes - 1)
        block = keys[pl.ds(row, body_rows), :]
        turned = pltpu.roll(block, (lanes - shift) & (lanes - 1), 1)
        merged = jnp.where(lane < lanes - shift, turned[:cap_rows], turned[1 : cap_rows + 1])
        out[o, 0:cap_rows, :] = merged
        head = jnp.zeros((1, lanes), i32)
        for p in range(pairs + 1):
            head = jnp.where(lane == p, starts[o * pairs + p] - off, head)
        out[o, cap_rows : cap_rows + 1, :] = head
        return carry

    lax.fori_loop(0, owners, one, 0)


def prep_kernel(row_bits, sample_bits, entries, rows_out, samples_out):
    e = entries[...]
    rows = e & ((1 << row_bits) - 1)
    lane = lax.broadcasted_iota(i32, e.shape, 1)
    place = lane & (group - 1)
    clash = jnp.zeros(e.shape, i32)
    for d in range(1, group):
        other = pltpu.roll(rows, lanes - d, 1)
        clash = jnp.where((other == rows) & (place < group - d), 1, clash)
    step = 1
    while step < group:
        clash = clash | pltpu.roll(clash, lanes - step, 1)
        step *= 2
    rows_out[...] = jnp.where(place == 0, rows | (clash << flag_bit), rows)
    samples_out[...] = lax.shift_right_logical(e, row_bits) & ((1 << sample_bits) - 1)


def one_hot(samples_ref, first_row, base, low, high, per_device, width):
    parts = []
    for c in range(width // lanes):
        s = samples_ref[pl.ds(first_row + c, 1), :]
        k = lax.broadcasted_iota(i32, (1, lanes), 1) + (base + c * lanes)
        s = jnp.where((k >= low) & (k < high), s, -1)
        hit = lax.broadcasted_iota(i32, (per_device, lanes), 0) == s
        parts.append(jnp.where(hit, 1.0, 0.0).astype(bf16))
    return parts[0] if len(parts) == 1 else jnp.concatenate(parts, axis=1)


def gather_kernel(ring, pair, pairs, per_device, cap, me, bounds, rows, samples, table, out, rows_f, stage):
    devices = out.shape[0] // per_device
    rows_own = table.shape[2]
    width = min(256, cap)
    unroll = 32
    mask = 2 * rows_own - 1
    lane = lax.broadcasted_iota(i32, (lanes, lanes), 1)
    cap_rows = cap // lanes

    def turn(c, carry):
        at = pl.multiple_of(c * lanes, lanes)
        t = table[0, :, pl.ds(at, lanes)].T
        rows_f[pl.ds(at, lanes), :] = jnp.where(lane < lanes // 2, t, 0.0)
        at_odd = pl.multiple_of(c * lanes + rows_own, lanes)
        rows_f[pl.ds(at_odd, lanes), :] = jnp.where(lane < lanes // 2, 0.0, t)
        return carry

    lax.fori_loop(0, rows_own // lanes, turn, 0)
    stage[...] = jnp.zeros(stage.shape, f32)

    def one(a, carry):
        sender = me[0] ^ ring.offset_of(a)
        low = bounds[sender * 8 + pair]
        high = bounds[sender * 8 + pair + 1]

        def fetch(i, c):
            at = pl.multiple_of(i * unroll, unroll)
            first = sender * cap + at
            for u in range(unroll):
                r = rows[first + u]
                if u % group == 0:
                    r = r & mask
                stage[pl.ds(at + u, 1), :] = rows_f[pl.ds(r, 1), :]
            return c

        lax.fori_loop(lax.shift_right_logical(low, 5), lax.shift_right_logical(high + 31, 5), fetch, 0)

        def fold(i, total):
            at = pl.multiple_of(i * width, width)
            hot = one_hot(samples, sender * cap_rows + i * (width // lanes), at, low, high, per_device, width)
            return total + jnp.dot(hot, stage[pl.ds(at, width), :].astype(bf16), preferred_element_type=f32)

        shift = bits_of(width)
        total = lax.fori_loop(
            lax.shift_right_logical(low, shift),
            lax.shift_right_logical(high + width - 1, shift),
            fold,
            jnp.zeros((per_device, lanes), f32),
        )
        out[pl.ds(pl.multiple_of(a * per_device, per_device), per_device), :] = total.astype(bf16)
        return carry

    lax.fori_loop(0, devices, one, 0)


def scatter_kernel(
    ring, pair, per_device, cap, me, bounds, rows, samples, grads, w_in, m_in, a_in,
    w_out, m_out, a_out, sums, stage, w_buf, m_buf, a_buf, in_sem, out_sem,
):
    devices = grads.shape[0] // per_device
    rows_own = w_in.shape[2]
    width = min(256, cap)
    mask = 2 * rows_own - 1
    cap_rows = cap // lanes
    sources = (w_in, m_in, a_in)
    targets = (w_out, m_out, a_out)
    buffers = (w_buf, m_buf, a_buf)
    for i in range(3):
        pltpu.make_async_copy(sources[i].at[pair], buffers[i], in_sem.at[i]).start()

    def wipe(c, carry):
        sums[pl.ds(pl.multiple_of(c * lanes, lanes), lanes), :] = jnp.zeros((lanes, lanes), f32)
        return carry

    lax.fori_loop(0, 2 * rows_own // lanes, wipe, 0)

    def one(a, carry):
        sender = me[0] ^ ring.offset_of(a)
        low = bounds[sender * 8 + pair]
        high = bounds[sender * 8 + pair + 1]
        mine = grads[pl.ds(pl.multiple_of(a * per_device, per_device), per_device), :]

        def spread(i, c):
            at = pl.multiple_of(i * width, width)
            hot = one_hot(samples, sender * cap_rows + i * (width // lanes), at, low, high, per_device, width)
            stage[pl.ds(at, width), :] = lax.dot_general(
                hot, mine, (((0,), (0,)), ((), ())), preferred_element_type=f32
            )
            return c

        shift = bits_of(width)
        lax.fori_loop(
            lax.shift_right_logical(low, shift), lax.shift_right_logical(high + width - 1, shift), spread, 0
        )

        def add(i, c):
            at = pl.multiple_of(i * group, group)
            first = sender * cap + at
            places = [rows[first + u] for u in range(group)]
            clash = lax.shift_right_logical(places[0], flag_bit)
            places[0] = places[0] & mask

            @pl.when(clash == 0)
            def _():
                olds = [sums[pl.ds(r, 1), :] for r in places]
                news = [stage[pl.ds(at + u, 1), :] for u in range(group)]
                for r, old, new in zip(places, olds, news):
                    sums[pl.ds(r, 1), :] = old + new

            @pl.when(clash != 0)
            def _():
                for u, r in enumerate(places):
                    sums[pl.ds(r, 1), :] = sums[pl.ds(r, 1), :] + stage[pl.ds(at + u, 1), :]

            return c

        lax.fori_loop(
            lax.shift_right_logical(low, bits_of(group)),
            lax.shift_right_logical(high + group - 1, bits_of(group)),
            add,
            0,
        )
        return carry

    lax.fori_loop(0, devices, one, 0)
    for i in range(3):
        pltpu.make_async_copy(sources[i].at[pair], buffers[i], in_sem.at[i]).wait()
    lane = lax.broadcasted_iota(i32, (lanes, lanes), 1)
    chunks = out_sem.shape[0] // 3
    chunk = rows_own // chunks

    def copies(n):
        span = pl.ds(n * chunk, chunk)
        return [
            pltpu.make_async_copy(buffers[i].at[:, span], targets[i].at[pair, :, span], out_sem.at[n * 3 + i])
            for i in range(3)
        ]

    for n in range(chunks):

        def update(c, carry):
            at = pl.multiple_of(n * chunk + c * lanes, lanes)
            even = sums[pl.ds(at, lanes), :]
            odd = sums[pl.ds(pl.multiple_of(at + rows_own, lanes), lanes), :]
            grad = jnp.where(lane < lanes // 2, even, odd).T
            span = (slice(None), pl.ds(at, lanes))
            new = nesterov(w_buf[span], m_buf[span], a_buf[span], grad, rates[0])
            w_buf[span] = new[0]
            m_buf[span] = new[1]
            a_buf[span] = new[2]
            return carry

        lax.fori_loop(0, chunk // lanes, update, 0)
        for copy in copies(n):
            copy.start()
    for n in range(chunks):
        for copy in copies(n):
            copy.wait()


def experts_forward(x_ref, w_in_ref, w_out_ref, y_ref, act_ref, slope_ref):
    w_in = w_in_ref[:, 0, 0].reshape(-1, w_in_ref.shape[-1])
    w_out = w_out_ref[:, 0, 0].reshape(-1, w_out_ref.shape[-1])
    hidden = jnp.dot(x_ref[...], w_in, preferred_element_type=f32)
    act, slope = gelu_pair(hidden)
    act = act.astype(bf16)
    act_ref[0, 0] = act
    slope_ref[0, 0] = slope.astype(bf16)
    term = lax.dot_general(act, w_out, (((1,), (1,)), ((), ())), preferred_element_type=f32)

    @pl.when(pl.program_id(1) == 0)
    def _():
        y_ref[0] = term

    @pl.when(pl.program_id(1) != 0)
    def _():
        y_ref[0] += term


def experts_backward(x_ref, d_ref, w_in_ref, w_out_ref, act_ref, slope_ref, dw_in_ref, dw_out_ref, dx_ref):
    w_in = w_in_ref[:, 0, 0].reshape(-1, w_in_ref.shape[-1])
    w_out = w_out_ref[:, 0, 0].reshape(-1, w_out_ref.shape[-1])
    d_out = d_ref[0]
    d_act = jnp.dot(d_out, w_out, preferred_element_type=f32)
    d_hidden = (d_act * slope_ref[0, 0].astype(f32)).astype(bf16)
    shape = (dw_in_ref.shape[0],) + dw_in_ref.shape[3:]
    first = (((0,), (0,)), ((), ()))
    dw_out = lax.dot_general(d_out, act_ref[0, 0], first, preferred_element_type=f32)
    dw_out_ref[:, 0, 0] = dw_out.astype(bf16).reshape(shape)
    dw_in = lax.dot_general(x_ref[...], d_hidden, first, preferred_element_type=f32)
    dw_in_ref[:, 0, 0] = dw_in.astype(bf16).reshape(shape)
    dx = lax.dot_general(d_hidden, w_in, (((1,), (1,)), ((), ())), preferred_element_type=f32)
    start = (pl.program_id(0) == 0) & (pl.program_id(1) == 0)

    @pl.when(start)
    def _():
        dx_ref[...] = dx

    @pl.when(jnp.logical_not(start))
    def _():
        dx_ref[...] += dx


def head_backward(x_rows, y_rows, label_rows, mask_rows, gate_low, tower_low, tower_v, sample_total):
    gate_logits = jnp.einsum("rf,kfe->rke", x_rows, gate_low, preferred_element_type=f32)
    gate_probs = jax.nn.softmax(gate_logits, axis=-1)
    mixture = jnp.einsum("rke,erf->rkf", gate_probs, y_rows, precision=highest).astype(bf16)
    tower_pre = jnp.einsum("rkf,kfc->rkc", mixture, tower_low, preferred_element_type=f32)
    tower_act, slopes = gelu_grad(tower_pre)
    logits = jnp.einsum("rkc,kc->rk", tower_act, tower_v, precision=highest)
    label_f = label_rows.astype(f32)
    weighting = jnp.asarray(task_weights, f32) * mask_rows.astype(f32)
    loss_part = jnp.sum(weighting * (jax.nn.softplus(logits) - label_f * logits))
    d_logits = weighting * (jax.nn.sigmoid(logits) - label_f) / sample_total
    d_tower_v = jnp.einsum("rk,rkc->kc", d_logits, tower_act, precision=highest)
    d_pre = (d_logits[:, :, None] * tower_v[None] * slopes).astype(bf16)
    d_tower_w = jnp.einsum("rkf,rkc->kfc", mixture, d_pre, preferred_element_type=f32)
    d_mixture = jnp.einsum("rkc,kfc->rkf", d_pre, tower_low, preferred_element_type=f32)
    d_probs = jnp.einsum("rkf,erf->rke", d_mixture, y_rows, precision=highest)
    d_logit_gate = (gate_probs * (d_probs - jnp.sum(gate_probs * d_probs, axis=-1, keepdims=True))).astype(bf16)
    d_expert = jnp.einsum("rke,rkf->erf", gate_probs, d_mixture, precision=highest).astype(bf16)
    d_gate_w = jnp.einsum("rf,rke->kfe", x_rows, d_logit_gate, preferred_element_type=f32)
    d_x_gate = jnp.einsum("rke,kfe->rf", d_logit_gate, gate_low, preferred_element_type=f32)
    return (loss_part, d_gate_w, d_tower_w, d_tower_v, d_x_gate, d_expert)


def smem():
    return pl.BlockSpec(memory_space=pltpu.SMEM)


def vmem():
    return pl.BlockSpec(memory_space=pltpu.VMEM)


def body(
    row_ids, bag_counts, labels, label_mask, tables, table_mom, table_avg, w_in, w_in_mom, w_in_avg,
    w_out, w_out_mom, w_out_avg, gate_w, gate_mom, gate_avg, tower_w, tower_w_mom, tower_w_avg,
    tower_v, tower_v_mom, tower_v_avg,
):
    n_model = lax.axis_size("mp")
    n_data = lax.axis_size("dp")
    devices = n_data * n_model
    ring = Ring(n_data, n_model)
    mp_rank = lax.axis_index("mp")
    me = (lax.axis_index("dp") * n_model + mp_rank).astype(i32).reshape(1)
    per_group, table_count, bag_size = row_ids.shape
    per_device = per_group // n_model
    rows_own = tables.shape[1]
    emb_width = tables.shape[2]
    features = table_count * emb_width
    pairs = features // lanes
    sample_total = float(per_group * n_data)
    slot_total = per_device * table_count * bag_size
    cap = 2 * slot_total // devices
    cap_rows = cap // lanes

    w_out_t, w_out_mom_t, w_out_avg_t = (v.transpose(0, 2, 1) for v in (w_out, w_out_mom, w_out_avg))
    experts, f_own, h_own = w_in.shape
    w_in_all = lax.all_gather(w_in.astype(bf16), both, axis=0).reshape(n_data, n_model, experts, f_own, h_own)
    w_out_all = lax.all_gather(w_out_t.astype(bf16), both, axis=0).reshape(n_data, n_model, experts, f_own, h_own)

    row_bits = bits_of(rows_own) + 1
    sample_bits = bits_of(per_device)
    start = mp_rank * per_device
    ids = lax.dynamic_slice_in_dim(row_ids.transpose(1, 2, 0), start, per_device, 2)
    counts = lax.dynamic_slice_in_dim(bag_counts.T, start, per_device, 1)
    live = lax.broadcasted_iota(i32, ids.shape, 1) < counts[:, None, :]
    table_of = lax.broadcasted_iota(i32, ids.shape, 0)
    bucket = lax.shift_right_logical(ids, row_bits - 1) * pairs + lax.shift_right_logical(table_of, 1)
    key = (bucket << sample_bits) | lax.broadcasted_iota(i32, ids.shape, 2)
    key = (((key << 1) | (table_of & 1)) << (row_bits - 1)) | (ids & (rows_own - 1))
    key = jnp.where(live, key, 1 << 30).reshape(-1)
    ordered = lax.sort(key)
    bucket_sorted = lax.shift_right_logical(ordered, row_bits + sample_bits)
    starts = jnp.sum(
        (bucket_sorted[None, :] < jnp.arange(devices * pairs + 1, dtype=i32)[:, None]).astype(i32), axis=1
    )
    padded = jnp.concatenate([ordered.reshape(-1, lanes), jnp.zeros((cap_rows + 8, lanes), i32)], axis=0)
    out_rows = -(-(cap_rows + 1) // 8) * 8
    outgoing = pl.pallas_call(
        functools.partial(bucket_kernel, pairs, cap_rows),
        out_shape=jax.ShapeDtypeStruct((devices, out_rows, lanes), i32),
        in_specs=[smem(), vmem()],
        out_specs=vmem(),
        name="bucket",
    )(starts, padded)
    received = lax.all_to_all(outgoing, both, split_axis=0, concat_axis=0, tiled=True)
    bounds = received[:, cap_rows, :8].reshape(-1)
    entries = received[:, :cap_rows].reshape(devices * cap_rows, lanes)
    entry_shape = jax.ShapeDtypeStruct(entries.shape, i32)
    rows, samples = pl.pallas_call(
        functools.partial(prep_kernel, row_bits, sample_bits),
        out_shape=(entry_shape, entry_shape),
        in_specs=[vmem()],
        out_specs=(vmem(), vmem()),
        name="prep",
    )(entries)
    rows = rows.reshape(-1)

    paired = tuple(
        v.transpose(0, 2, 1).reshape(pairs, lanes, rows_own) for v in (tables, table_mom, table_avg)
    )
    pieces = []
    for pair in range(pairs):
        partial_sums = pl.pallas_call(
            functools.partial(gather_kernel, ring, pair, pairs, per_device, cap),
            grid=(1,),
            out_shape=jax.ShapeDtypeStruct((devices * per_device, lanes), bf16),
            in_specs=[
                smem(), smem(), smem(), vmem(),
                pl.BlockSpec((1, lanes, rows_own), lambda i, pair=pair: (pair, 0, 0)),
            ],
            out_specs=vmem(),
            scratch_shapes=[pltpu.VMEM((2 * rows_own, lanes), f32), pltpu.VMEM((cap, lanes), f32)],
            compiler_params=params(),
            name="gather",
        )(me, bounds, rows, samples, paired[0])
        pieces.append(ring.reduce_scatter(partial_sums.reshape(devices, per_device, lanes)))
    inverse = jnp.repeat(1.0 / counts.T.astype(f32), emb_width, axis=1)
    x = (jnp.concatenate(pieces, axis=1) * inverse).astype(bf16)

    hidden_shape = jax.ShapeDtypeStruct((experts, n_model, per_device, h_own), bf16)
    weight_spec = pl.BlockSpec((n_data, 1, 1, f_own, h_own), lambda e, m: (0, m, e, 0, 0))
    hidden_spec = pl.BlockSpec((1, 1, per_device, h_own), lambda e, m: (e, m, 0, 0))
    expert_spec = pl.BlockSpec((1, per_device, features), lambda e, m: (e, 0, 0))
    whole_spec = pl.BlockSpec((per_device, features), lambda e, m: (0, 0))
    y, act, slope = pl.pallas_call(
        experts_forward,
        grid=(experts, n_model),
        out_shape=(jax.ShapeDtypeStruct((experts, per_device, features), f32), hidden_shape, hidden_shape),
        in_specs=[whole_spec, weight_spec, weight_spec],
        out_specs=(expert_spec, hidden_spec, hidden_spec),
        compiler_params=params(),
        name="experts_forward",
    )(x, w_in_all, w_out_all)
    gate_low = gate_w.astype(bf16)
    tower_low = tower_w.astype(bf16)
    label_rows = lax.dynamic_slice_in_dim(labels, start, per_device, 0)
    mask_rows = lax.dynamic_slice_in_dim(label_mask, start, per_device, 0)
    loss_part, d_gate_w, d_tower_w, d_tower_v, d_x_gate, d_expert = head_backward(
        x, y, label_rows, mask_rows, gate_low, tower_low, tower_v, sample_total
    )
    weight_shape = jax.ShapeDtypeStruct((n_data, n_model, experts, f_own, h_own), bf16)
    dw_in, dw_out, d_x = pl.pallas_call(
        experts_backward,
        grid=(experts, n_model),
        out_shape=(weight_shape, weight_shape, jax.ShapeDtypeStruct((per_device, features), f32)),
        in_specs=[whole_spec, expert_spec, weight_spec, weight_spec, hidden_spec, hidden_spec],
        out_specs=(weight_spec, weight_spec, whole_spec),
        compiler_params=params(),
        name="experts_backward",
    )(x, d_expert, w_in_all, w_out_all, act, slope)
    outgoing_grads = ((d_x + d_x_gate) * inverse).astype(bf16)

    table_outs = None
    paired_shape = jax.ShapeDtypeStruct(paired[0].shape, f32)
    for pair in range(pairs):
        gathered = ring.all_gather(outgoing_grads[:, pair * lanes : (pair + 1) * lanes])
        gathered = gathered.reshape(devices * per_device, lanes)
        hbm = pl.BlockSpec(memory_space=pl.ANY)
        chunks = 4
        operands = (me, bounds, rows, samples, gathered) + paired
        call = functools.partial(scatter_kernel, ring, pair, per_device, cap)
        in_specs = [smem(), smem(), smem(), vmem(), vmem(), hbm, hbm, hbm]
        aliases = {}
        if table_outs is not None:
            operands = operands + table_outs
            in_specs = in_specs + [hbm, hbm, hbm]
            aliases = {8: 0, 9: 1, 10: 2}
            call = functools.partial(skip_old, call)
        table_outs = pl.pallas_call(
            call,
            out_shape=(paired_shape,) * 3,
            in_specs=in_specs,
            out_specs=(hbm, hbm, hbm),
            scratch_shapes=[
                pltpu.VMEM((2 * rows_own, lanes), f32),
                pltpu.VMEM((cap, lanes), f32),
                pltpu.VMEM((lanes, rows_own), f32),
                pltpu.VMEM((lanes, rows_own), f32),
                pltpu.VMEM((lanes, rows_own), f32),
                pltpu.SemaphoreType.DMA((3,)),
                pltpu.SemaphoreType.DMA((3 * chunks,)),
            ],
            input_output_aliases=aliases,
            compiler_params=params(),
            name="scatter",
        )(*operands)
    table_new = tuple(v.reshape(table_count, emb_width, rows_own).transpose(0, 2, 1) for v in table_outs)

    loss_sum, d_gate_w, d_tower_w, d_tower_v = lax.psum((loss_part, d_gate_w, d_tower_w, d_tower_v), both)
    own = (devices, experts, f_own, h_own)
    d_w_in = lax.psum_scatter(dw_in.reshape(own), both, scatter_dimension=0, tiled=True)[0].astype(f32)
    d_w_out = lax.psum_scatter(dw_out.reshape(own), both, scatter_dimension=0, tiled=True)[0].astype(f32)
    w_in_new = nesterov(w_in, w_in_mom, w_in_avg, d_w_in, rates[1])
    w_out_new = nesterov(w_out_t, w_out_mom_t, w_out_avg_t, d_w_out, rates[2])
    w_out_new = tuple(v.transpose(0, 2, 1) for v in w_out_new)
    gate_new = nesterov(gate_w, gate_mom, gate_avg, d_gate_w, rates[3])
    tower_new = nesterov(tower_w, tower_w_mom, tower_w_avg, d_tower_w, rates[4])
    vector_new = nesterov(tower_v, tower_v_mom, tower_v_avg, d_tower_v, rates[5])
    return (loss_sum,) + table_new + w_in_new + w_out_new + gate_new + tower_new + vector_new


def skip_old(call, me, bounds, rows, samples, grads, w, m, a, old_w, old_m, old_a, *rest):
    call(me, bounds, rows, samples, grads, w, m, a, *rest)


def solution(mesh):
    group_spec = P("dp", None)
    table_spec = P(None, both, None)
    placed = (
        (P("dp", None, None), group_spec, group_spec, group_spec)
        + (table_spec,) * 3
        + (P(None, "dp", "mp"),) * 3
        + (P(None, "mp", "dp"),) * 3
        + (P(),) * 9
    )
    return jax.shard_map(
        body,
        mesh=mesh,
        in_specs=placed,
        out_specs=(P(),)
        + (table_spec,) * 3
        + (P(None, "dp", "mp"),) * 3
        + (P(None, "mp", "dp"),) * 3
        + (P(),) * 9,
        check_vma=False,
    )
```

time: 2500 us -> 810 us (0.32)
  local copies, waits for them, and re-layouts: 1240 us -> 44.9 us
  other arithmetic: 508 us -> 41.9 us
  Pallas kernels: 0 us -> 334 us
  waiting for transfers between devices: 399 us -> 195 us
  blocking collectives: 220 us -> 40.8 us
  starting transfers between devices: 20.1 us -> 92.4 us
  matrix products: 80.2 us -> 34.6 us
    gather x5 -> x0, local copies, waits for them, and re-layouts: 949 us -> none  [the longest x1 363 us: body(): local_row[source]]
    scatter-add x1 -> x0, other arithmetic: 414 us -> none  [body(): d_tables = jnp.zeros((table_count * rows_own, emb_width), jnp.float32).at...]
    pallas_call x0 -> x12, Pallas kernels: none -> 334 us  [the longest x4 156 us: body(): pl.pallas_call(call, out_shape=(paired_shape,) * 3, in_specs=in_specs, ou...]
    all_to_all x3 -> x1, waiting for transfers between devices: 206 us -> 19.8 us  [body(): lax.all_to_all(outgoing, both, split_axis=0, concat_axis=0, tiled=True)]
    psum x1, blocking collectives: 220 us -> 40.8 us  [body(): lax.psum((loss_part, d_gate_w, d_tower_w, d_tower_v), both)]
    all_gather x4 -> x2, waiting for transfers between devices: 124 us -> 0.04 us  [the longest x1 0.02 us: body(): lax.all_gather(w_in.astype(bf16), both, axis=0)]
    scatter x1 -> x0, local copies, waits for them, and re-layouts: 120 us -> none  [body(): filler = jnp.full((owner_total * capacity,), -1, jnp.int32).at[bucket].se...]
    ppermute x0 -> x48, waiting for transfers between devices: none -> 105 us  [swap(): lax.ppermute(value, axis, [(i, i ^ distance * stride) for i in range(coun...]
  transfers between devices with their start and end apart: 12 -> 54, of which waited for: 5 -> 19; matrix products, arithmetic and copies ran while one was open for 19% -> 10% of each run, Pallas kernels for 0% -> 38%
where the time goes in v1:
time: 810 us; the launch traced here: 799 us
  Pallas kernels  334 us (41%)
  waiting for transfers between devices  195 us (24%)
  starting transfers between devices  92.4 us (11%)
  local copies, waits for them, and re-layouts  44.9 us (6%)
  other arithmetic  41.9 us (5%)
  blocking collectives  40.8 us (5%)
  matrix products  34.6 us (4%)
  between operations  15.2 us (2%)
    pallas_call x4, Pallas kernels, body(): pl.pallas_call(call, out_shape=(paired_shape,) * 3, in_specs=in_specs, ou...  156 us
    pallas_call x4, Pallas kernels, body(): pl.pallas_call(functools.partial(gather_kernel, ring, pair, pairs, per_de...  106 us
    ppermute x48, waiting for transfers between devices, swap(): lax.ppermute(value, axis, [(i, i ^ distance * stride) for i in range(coun...  105 us
    ppermute x48, starting transfers between devices, swap(): lax.ppermute(value, axis, [(i, i ^ distance * stride) for i in range(coun...  84.9 us
    reduce_scatter x1, waiting for transfers between devices, body(): lax.psum_scatter(dw_in.reshape(own), both, scatter_dimension=0, tiled=True)  69.7 us
    psum x1, blocking collectives, body(): lax.psum((loss_part, d_gate_w, d_tower_w, d_tower_v), both)  40.8 us
    pallas_call x1, Pallas kernels, body(): pl.pallas_call(experts_backward, grid=(experts, n_model), out_shape=(weig...  33.1 us
    pallas_call x1, Pallas kernels, body(): pl.pallas_call(experts_forward, grid=(experts, n_model), out_shape=(jax.S...  31.5 us
  transfers between devices with their start and end apart: 54, of which 19 were waited for; matrix products, arithmetic and copies ran while one was open for 10% of the time, Pallas kernels for 38%

profile of v1, /device:TPU:0, one launch (start us, length us, event | category | flops | bytes accessed | tf_op | source)
XLA Modules:
  0.0 798.7 jit_solution(1655587589988250392)
XLA Ops:
  12.1 11.2 %sort.14 = (s32[32768]{0:T(1024)S(1)}, s32[32768]{0:T(1024)}) sort(s32[32768]{0:T(1024)S(1)} %bitcast.264, s32[32768]{0:T(1024)S(1)} %iota.33), dimensions={0}, to_apply=%region_0.1 | sort | flops 491520 | bytes 524288 | tf_op jit(solution)/shard_map/sort | solution.py:419
  31.1 7.3 all-to-all-start
  38.4 19.8 %all-to-all-done = s32[32,24,128]{2,1,0:T(8,128)S(1)} async-done(((s32[32,24,128]{2,1,0:T(8,128)}), s32[32,24,128]{2,1,0:T(8,128)S(1)}, u32[]{:S(2)}, u32[]{:S(2)}) %all-to-all-start) | async-done | bytes 393248 | tf_op jit(solution)/shard_map/all_to_all | solution.py:433
  62.9 28.2 %gather.7 = bf16[8192,128]{1,0:T(8,128)(2,1)} custom-call(s32[1]{0:T(128)} %bitcast.me, s32[256]{0:T(256)} %reshape_squeeze.3.bounds, s32[65536]{0:T(1024)} %bitcast.242, s32[512,128]{1,0:T(8,128)} %get-tuple-element.43.samples, f32[4,128,8192]{2,1,0:T(8,128)} %bitcast.219), custom_call_target="tpu_custom_call" | custom-call | tf_op jit(solution)/shard_map/gather/pallas_call | solution.py:451
  91.2 25.8 %gather.6 = bf16[8192,128]{1,0:T(8,128)(2,1)} custom-call(s32[1]{0:T(128)} %bitcast.me, s32[256]{0:T(256)} %reshape_squeeze.3.bounds, s32[65536]{0:T(1024)} %bitcast.243, s32[512,128]{1,0:T(8,128)} %get-tuple-element.43.samples, f32[4,128,8192]{2,1,0:T(8,128)} %bitcast.220), custom_call_target="tpu_custom_call" | custom-call | tf_op jit(solution)/shard_map/gather/pallas_call | solution.py:451
  117.0 28.4 %gather.5 = bf16[8192,128]{1,0:T(8,128)(2,1)} custom-call(s32[1]{0:T(128)} %bitcast.me, s32[256]{0:T(256)} %reshape_squeeze.3.bounds, s32[65536]{0:T(1024)} %bitcast.244, s32[512,128]{1,0:T(8,128)} %get-tuple-element.43.samples, f32[4,128,8192]{2,1,0:T(8,128)} %bitcast.221), custom_call_target="tpu_custom_call" | custom-call | tf_op jit(solution)/shard_map/gather/pallas_call | solution.py:451
  145.4 23.9 %gather.4 = bf16[8192,128]{1,0:T(8,128)(2,1)} custom-call(s32[1]{0:T(128)} %bitcast.me, s32[256]{0:T(256)} %reshape_squeeze.3.bounds, s32[65536]{0:T(1024)} %bitcast.245, s32[512,128]{1,0:T(8,128)} %get-tuple-element.43.samples, f32[4,128,8192]{2,1,0:T(8,128)} %bitcast.222), custom_call_target="tpu_custom_call" | custom-call | tf_op jit(solution)/shard_map/gather/pallas_call | solution.py:451
  195.6 8.8 %collective-permute-done.13 = bf16[8,256,128]{2,1,0:T(8,128)(2,1)S(1)} collective-permute-done((bf16[8,256,128]{2,1,0:T(8,128)(2,1)S(1)}, bf16[8,256,128]{2,1,0:T(8,128)(2,1)S(1)}, u32[]{:S(2)}, u32[]{:S(2)}) %collective-permute-start.13) | collective-permute-done | bytes 524320 | tf_op jit(solution)/shard_map/ppermute | solution.py:73
  206.8 8.8 %collective-permute-done.7 = bf16[8,256,128]{2,1,0:T(8,128)(2,1)S(1)} collective-permute-done((bf16[8,256,128]{2,1,0:T(8,128)(2,1)S(1)}, bf16[8,256,128]{2,1,0:T(8,128)(2,1)S(1)}, u32[]{:S(2)}, u32[]{:S(2)}) %collective-permute-start.7) | collective-permute-done | bytes 524320 | tf_op jit(solution)/shard_map/ppermute | solution.py:73
  218.1 8.4 %collective-permute-done.1 = bf16[8,256,128]{2,1,0:T(8,128)(2,1)S(1)} collective-permute-done((bf16[8,256,128]{2,1,0:T(8,128)(2,1)S(1)}, bf16[8,256,128]{2,1,0:T(8,128)(2,1)S(1)}, u32[]{:S(2)}, u32[]{:S(2)}) %collective-permute-start.1) | collective-permute-done | bytes 524320 | tf_op jit(solution)/shard_map/ppermute | solution.py:73
  229.0 28.9 %collective-permute-start.21 = (bf16[1,256,128]{2,1,0:T(8,128)(2,1)S(1)}, bf16[1,256,128]{2,1,0:T(8,128)(2,1)S(1)}, u32[]{:S(2)}, u32[]{:S(2)}) collective-permute-start(bf16[1,256,128]{2,1,0:T(8,128)(2,1)S(1)} %get-tuple-element.134), channel_id=1, source_target_pairs={{0,8},{4,12},{8,0},{12,4},{16,24},{20,28},{24,16},{28,20},{1,9},{5... | collective-permute-start | bytes 196616 | tf_op jit(solution)/shard_map/ppermute | solution.py:73
  283.5 31.5 %experts_forward.1 = (f32[8,256,512]{2,1,0:T(8,128)}, bf16[8,4,256,256]{3,2,1,0:T(8,128)(2,1)}, bf16[8,4,256,256]{3,2,1,0:T(8,128)(2,1)}) custom-call(bf16[256,512]{1,0:T(8,128)(2,1)} %copy-done.8, bf16[8,4,8,64,256]{4,3,2,1,0:T(8,128)(2,1)} %bitcast.238, bf16[8,4,8,64,256]{4,3,2,1,0:T(8,128)(2,1)} %bitcast.240), custom_call_target="tpu_custom_call" | custom-call | tf_op jit(solution)/shard_map/experts_forward/pallas_call | solution.py:473
  314.9 8.6 %fusion.6 = bf16[256,5,512]{2,1,0:T(8,128)(2,1)S(1)} fusion(f32[256,5,8]{1,2,0:T(8,128)S(1)} %copy.107, f32[8,256,512]{2,1,0:T(8,128)} %get-tuple-element.44), kind=kOutput, calls=%fused_computation.9 | convolution fusion | flops 62914560 | bytes 5545984 | tf_op jit(solution)/shard_map/rke,erf->rkf/dot_general | solution.py:353
  331.3 12.7 %fusion.1 = f32[256,5,8]{2,1,0:T(8,128)} fusion(f32[256,5,512]{2,0,1:T(8,128)S(1)} %convolution_bitcast_fusion, f32[8,256,512]{2,1,0:T(8,128)S(1)} %copy-done), kind=kOutput, calls=%fused_computation.3 | convolution fusion | flops 62914560 | bytes 6856704 | tf_op jit(solution)/shard_map/rkf,erf->rke/dot_general | solution.py:365
  357.3 33.1 %experts_backward.1 = (bf16[8,4,8,64,256]{4,3,2,1,0:T(8,128)(2,1)}, bf16[8,4,8,64,256]{4,3,2,1,0:T(8,128)(2,1)}, f32[256,512]{1,0:T(8,128)}) custom-call(bf16[256,512]{1,0:T(8,128)(2,1)} %copy-done.8, bf16[8,256,512]{2,1,0:T(8,128)(2,1)} %bitcast.252, bf16[8,4,8,64,256]{4,3,2,1,0:T(8,128)(2,1)} %bitcast.239, bf16[8,4,8,64,256]{4,3,2,1,0:T(8,128)(2,1)} %bitcast.241, ...), custom_call_target="tpu_custom_call" | custom-call | tf_op jit(solution)/shard_map/experts_backward/pallas_call | solution.py:490
  400.0 40.8 %all-reduce.1 = (f32[]{:T(128)}, f32[5,128]{1,0:T(8,128)}) all-reduce(f32[]{:T(128)} %get-tuple-element.138, f32[5,128]{1,0:T(8,128)S(1)} %bitcast.267), channel_id=1, replica_groups=mesh['dp'=8,'mp'=4] {'dp','mp'}, use_global_device_ids=true, to_apply=%region_5.6 | all-reduce | flops 641 | bytes 5128 | tf_op jit(solution)/shard_map/psum | solution.py:537
  486.0 14.9 %collective-permute-done.40 = bf16[8,256,128]{2,1,0:T(8,128)(2,1)S(1)} collective-permute-done((bf16[8,256,128]{2,1,0:T(8,128)(2,1)S(1)}, bf16[8,256,128]{2,1,0:T(8,128)(2,1)S(1)}, u32[]{:S(2)}, u32[]{:S(2)}) %collective-permute-start.40) | collective-permute-done | bytes 524320 | tf_op jit(solution)/shard_map/ppermute | solution.py:73
  502.1 21.3 %collective-permute-done.34 = bf16[8,256,128]{2,1,0:T(8,128)(2,1)S(1)} collective-permute-done((bf16[8,256,128]{2,1,0:T(8,128)(2,1)S(1)}, bf16[8,256,128]{2,1,0:T(8,128)(2,1)S(1)}, u32[]{:S(2)}, u32[]{:S(2)}) %collective-permute-start.34) | collective-permute-done | bytes 524320 | tf_op jit(solution)/shard_map/ppermute | solution.py:73
  524.6 18.4 %collective-permute-done.28 = bf16[8,256,128]{2,1,0:T(8,128)(2,1)S(1)} collective-permute-done((bf16[8,256,128]{2,1,0:T(8,128)(2,1)S(1)}, bf16[8,256,128]{2,1,0:T(8,128)(2,1)S(1)}, u32[]{:S(2)}, u32[]{:S(2)}) %collective-permute-start.28) | collective-permute-done | bytes 524320 | tf_op jit(solution)/shard_map/ppermute | solution.py:73
  553.0 35.3 %scatter.4 = (f32[4,128,8192]{2,1,0:T(8,128)}, f32[4,128,8192]{2,1,0:T(8,128)}, f32[4,128,8192]{2,1,0:T(8,128)}) custom-call(s32[1]{0:T(128)} %bitcast.me, s32[256]{0:T(256)} %reshape_squeeze.3.bounds, s32[65536]{0:T(1024)} %bitcast.246, s32[512,128]{1,0:T(8,128)} %get-tuple-element.43.samples, bf16[8192,128]{1,0:T(8,128)(2,1)} %bitcast.260, ...), custom_call_target="tpu_custom_call" | custom-call | tf_op jit(solution)/shard_map/scatter/pallas_call | solution.py:517
  591.0 41.4 %scatter.5 = (f32[4,128,8192]{2,1,0:T(8,128)}, f32[4,128,8192]{2,1,0:T(8,128)}, f32[4,128,8192]{2,1,0:T(8,128)}) custom-call(s32[1]{0:T(128)} %bitcast.me, s32[256]{0:T(256)} %reshape_squeeze.3.bounds, s32[65536]{0:T(1024)} %bitcast.247, s32[512,128]{1,0:T(8,128)} %get-tuple-element.43.samples, ...), custom_call_target="tpu_custom_call", output_to_operand_aliasing={{0}: (8, {}), {1}: (9, {}), {2}: (10, {})} | custom-call | tf_op jit(solution)/shard_map/scatter/pallas_call | solution.py:517
  635.2 38.0 %scatter.6 = (f32[4,128,8192]{2,1,0:T(8,128)}, f32[4,128,8192]{2,1,0:T(8,128)}, f32[4,128,8192]{2,1,0:T(8,128)}) custom-call(s32[1]{0:T(128)} %bitcast.me, s32[256]{0:T(256)} %reshape_squeeze.3.bounds, s32[65536]{0:T(1024)} %bitcast.248, s32[512,128]{1,0:T(8,128)} %get-tuple-element.43.samples, ...), custom_call_target="tpu_custom_call", output_to_operand_aliasing={{0}: (8, {}), {1}: (9, {}), {2}: (10, {})} | custom-call | tf_op jit(solution)/shard_map/scatter/pallas_call | solution.py:517
  675.9 41.3 %scatter.7 = (f32[4,128,8192]{2,1,0:T(8,128)}, f32[4,128,8192]{2,1,0:T(8,128)}, f32[4,128,8192]{2,1,0:T(8,128)}) custom-call(s32[1]{0:T(128)} %bitcast.me, s32[256]{0:T(256)} %reshape_squeeze.3.bounds, s32[65536]{0:T(1024)} %bitcast.249, s32[512,128]{1,0:T(8,128)} %get-tuple-element.43.samples, ...), custom_call_target="tpu_custom_call", output_to_operand_aliasing={{0}: (8, {}), {1}: (9, {}), {2}: (10, {})} | custom-call | tf_op jit(solution)/shard_map/scatter/pallas_call | solution.py:517
  719.8 69.7 %reduce-scatter.3.cloned.1.call-done = bf16[1,8,64,256]{3,2,1,0:T(8,128)(2,1)} async-done(((bf16[32,8,64,256]{3,2,1,0:T(8,128)(2,1)}), bf16[1,8,64,256]{3,2,1,0:T(8,128)(2,1)}) %reduce-scatter.3.cloned.1.call-update) | async-done | bytes 262160 | tf_op jit(solution)/shard_map/reduce_scatter | solution.py:539
  (292 shorter events, 177.1 us)
Async XLA Ops:
  7.2 276.2 %all-gather.5.cloned.1.call-start = ((), (), s32[]{:S(2)}) async-start(), calls=%async_computation.5 | async-start | bytes 8650752 | tf_op jit(solution)/shard_map/all_gather | solution.py:405
  9.0 274.4 %all-gather.7.cloned.1.call-start = ((), (), s32[]{:S(2)}) async-start(), calls=%async_computation.6 | async-start | bytes 8650752 | tf_op jit(solution)/shard_map/all_gather | solution.py:406
  38.4 505.7 %all-reduce.5.cloned.1.call-start = ((), (), s32[]{:S(2)}) async-start(), calls=%async_computation.7 | async-start | bytes 2785280 | tf_op jit(solution)/shard_map/psum | solution.py:537
  183.7 32.0 %collective-permute-start.7 = (bf16[8,256,128]{2,1,0:T(8,128)(2,1)S(1)}, bf16[8,256,128]{2,1,0:T(8,128)(2,1)S(1)}, u32[]{:S(2)}, u32[]{:S(2)}) collective-permute-start(bf16[8,256,128]{2,1,0:T(8,128)(2,1)S(1)} %slice.239), channel_id=1, source_target_pairs={{0,2},{1,3},{2,0},{3,1},{4,6},{5,7},{6,4},{7,5},{8,10},{9,11},{10,... | collective-permute-start | bytes 1572872 | tf_op jit(solution)/shard_map/ppermute | solution.py:73
  187.3 39.2 %collective-permute-start.1 = (bf16[8,256,128]{2,1,0:T(8,128)(2,1)S(1)}, bf16[8,256,128]{2,1,0:T(8,128)(2,1)S(1)}, u32[]{:S(2)}, u32[]{:S(2)}) collective-permute-start(bf16[8,256,128]{2,1,0:T(8,128)(2,1)S(1)} %slice.229), channel_id=1, source_target_pairs={{0,2},{1,3},{2,0},{3,1},{4,6},{5,7},{6,4},{7,5},{8,10},{9,11},{10,... | collective-permute-start | bytes 1572872 | tf_op jit(solution)/shard_map/ppermute | solution.py:73
  193.3 35.6 %collective-permute-start.20 = (bf16[4,256,128]{2,1,0:T(8,128)(2,1)S(1)}, bf16[4,256,128]{2,1,0:T(8,128)(2,1)S(1)}, u32[]{:S(2)}, u32[]{:S(2)}) collective-permute-start(bf16[4,256,128]{2,1,0:T(8,128)(2,1)S(1)} %slice.261), channel_id=1, source_target_pairs={{0,4},{4,0},{8,12},{12,8},{16,20},{20,16},{24,28},{28,24},{1,5},{5... | collective-permute-start | bytes 786440 | tf_op jit(solution)/shard_map/ppermute | solution.py:73
  204.6 53.3 %collective-permute-start.14 = (bf16[4,256,128]{2,1,0:T(8,128)(2,1)S(1)}, bf16[4,256,128]{2,1,0:T(8,128)(2,1)S(1)}, u32[]{:S(2)}, u32[]{:S(2)}) collective-permute-start(bf16[4,256,128]{2,1,0:T(8,128)(2,1)S(1)} %slice.251), channel_id=1, source_target_pairs={{0,4},{4,0},{8,12},{12,8},{16,20},{20,16},{24,28},{28,24},{1,5},{5... | collective-permute-start | bytes 786440 | tf_op jit(solution)/shard_map/ppermute | solution.py:73
  215.8 43.7 %collective-permute-start.8 = (bf16[4,256,128]{2,1,0:T(8,128)(2,1)S(1)}, bf16[4,256,128]{2,1,0:T(8,128)(2,1)S(1)}, u32[]{:S(2)}, u32[]{:S(2)}) collective-permute-start(bf16[4,256,128]{2,1,0:T(8,128)(2,1)S(1)} %slice.241), channel_id=1, source_target_pairs={{0,4},{4,0},{8,12},{12,8},{16,20},{20,16},{24,28},{28,24},{1,5},{5... | collective-permute-start | bytes 786440 | tf_op jit(solution)/shard_map/ppermute | solution.py:73
  226.7 35.9 %collective-permute-start.2 = (bf16[4,256,128]{2,1,0:T(8,128)(2,1)S(1)}, bf16[4,256,128]{2,1,0:T(8,128)(2,1)S(1)}, u32[]{:S(2)}, u32[]{:S(2)}) collective-permute-start(bf16[4,256,128]{2,1,0:T(8,128)(2,1)S(1)} %slice.231), channel_id=1, source_target_pairs={{0,4},{4,0},{8,12},{12,8},{16,20},{20,16},{24,28},{28,24},{1,5},{5... | collective-permute-start | bytes 786440 | tf_op jit(solution)/shard_map/ppermute | solution.py:73
  229.0 33.8 %collective-permute-start.21 = (bf16[1,256,128]{2,1,0:T(8,128)(2,1)S(1)}, bf16[1,256,128]{2,1,0:T(8,128)(2,1)S(1)}, u32[]{:S(2)}, u32[]{:S(2)}) collective-permute-start(bf16[1,256,128]{2,1,0:T(8,128)(2,1)S(1)} %get-tuple-element.134), channel_id=1, source_target_pairs={{0,8},{4,12},{8,0},{12,4},{16,24},{20,28},{24,16},{28,20},{1,9},{5... | collective-permute-start | bytes 196616 | tf_op jit(solution)/shard_map/ppermute | solution.py:73
  348.5 368.7 %reduce-scatter.5.cloned.1.call-start = ((), (), s32[]{:S(2)}) async-start(), calls=%async_computation.4 | async-start | bytes 8650752 | tf_op jit(solution)/shard_map/reduce_scatter | solution.py:540
  390.4 399.1 %reduce-scatter.3.cloned.1.call-start = ((), (), s32[]{:S(2)}) async-start(), calls=%async_computation.3 | async-start | bytes 8650752 | tf_op jit(solution)/shard_map/reduce_scatter | solution.py:539
  391.9 52.5 %collective-permute-start.44 = (bf16[1,256,128]{2,1,0:T(8,128)(2,1)S(1)}, bf16[1,256,128]{2,1,0:T(8,128)(2,1)S(1)}, u32[]{:S(2)}, u32[]{:S(2)}) collective-permute-start(bf16[1,256,128]{2,1,0:T(8,128)(2,1)S(1)} %get-tuple-element.112), channel_id=1, source_target_pairs={{0,24},{4,28},{8,16},{12,20},{16,8},{20,12},{24,0},{28,4},{1,25},{... | collective-permute-start | bytes 196616 | tf_op jit(solution)/shard_map/ppermute | solution.py:73
  394.1 51.4 %collective-permute-start.43 = (bf16[1,256,128]{2,1,0:T(8,128)(2,1)S(1)}, bf16[1,256,128]{2,1,0:T(8,128)(2,1)S(1)}, u32[]{:S(2)}, u32[]{:S(2)}) collective-permute-start(bf16[1,256,128]{2,1,0:T(8,128)(2,1)S(1)} %get-tuple-element.112), channel_id=1, source_target_pairs={{0,16},{4,20},{8,24},{12,28},{16,0},{20,4},{24,8},{28,12},{1,17},{... | collective-permute-start | bytes 196616 | tf_op jit(solution)/shard_map/ppermute | solution.py:73
  394.1 46.7 %collective-permute-start.38 = (bf16[1,256,128]{2,1,0:T(8,128)(2,1)S(1)}, bf16[1,256,128]{2,1,0:T(8,128)(2,1)S(1)}, u32[]{:S(2)}, u32[]{:S(2)}) collective-permute-start(bf16[1,256,128]{2,1,0:T(8,128)(2,1)S(1)} %get-tuple-element.113), channel_id=1, source_target_pairs={{0,24},{4,28},{8,16},{12,20},{16,8},{20,12},{24,0},{28,4},{1,25},{... | collective-permute-start | bytes 196616 | tf_op jit(solution)/shard_map/ppermute | solution.py:73
  395.8 45.3 %collective-permute-start.37 = (bf16[1,256,128]{2,1,0:T(8,128)(2,1)S(1)}, bf16[1,256,128]{2,1,0:T(8,128)(2,1)S(1)}, u32[]{:S(2)}, u32[]{:S(2)}) collective-permute-start(bf16[1,256,128]{2,1,0:T(8,128)(2,1)S(1)} %get-tuple-element.113), channel_id=1, source_target_pairs={{0,16},{4,20},{8,24},{12,28},{16,0},{20,4},{24,8},{28,12},{1,17},{... | collective-permute-start | bytes 196616 | tf_op jit(solution)/shard_map/ppermute | solution.py:73
  397.8 45.4 %collective-permute-start.36 = (bf16[1,256,128]{2,1,0:T(8,128)(2,1)S(1)}, bf16[1,256,128]{2,1,0:T(8,128)(2,1)S(1)}, u32[]{:S(2)}, u32[]{:S(2)}) collective-permute-start(bf16[1,256,128]{2,1,0:T(8,128)(2,1)S(1)} %get-tuple-element.113), channel_id=1, source_target_pairs={{0,8},{4,12},{8,0},{12,4},{16,24},{20,28},{24,16},{28,20},{1,9},{5... | collective-permute-start | bytes 196616 | tf_op jit(solution)/shard_map/ppermute | solution.py:73
  473.4 27.5 %collective-permute-start.40 = (bf16[8,256,128]{2,1,0:T(8,128)(2,1)S(1)}, bf16[8,256,128]{2,1,0:T(8,128)(2,1)S(1)}, u32[]{:S(2)}, u32[]{:S(2)}) collective-permute-start(bf16[8,256,128]{2,1,0:T(8,128)(2,1)S(1)} %get-tuple-element.118), channel_id=1, source_target_pairs={{0,2},{1,3},{2,0},{3,1},{4,6},{5,7},{6,4},{7,5},{8,10},{9,11},{10,... | collective-permute-start | bytes 1572872 | tf_op jit(solution)/shard_map/ppermute | solution.py:73
  477.7 45.6 %collective-permute-start.34 = (bf16[8,256,128]{2,1,0:T(8,128)(2,1)S(1)}, bf16[8,256,128]{2,1,0:T(8,128)(2,1)S(1)}, u32[]{:S(2)}, u32[]{:S(2)}) collective-permute-start(bf16[8,256,128]{2,1,0:T(8,128)(2,1)S(1)} %get-tuple-element.121), channel_id=1, source_target_pairs={{0,2},{1,3},{2,0},{3,1},{4,6},{5,7},{6,4},{7,5},{8,10},{9,11},{10,... | collective-permute-start | bytes 1572872 | tf_op jit(solution)/shard_map/ppermute | solution.py:73
  480.5 62.5 %collective-permute-start.28 = (bf16[8,256,128]{2,1,0:T(8,128)(2,1)S(1)}, bf16[8,256,128]{2,1,0:T(8,128)(2,1)S(1)}, u32[]{:S(2)}, u32[]{:S(2)}) collective-permute-start(bf16[8,256,128]{2,1,0:T(8,128)(2,1)S(1)} %get-tuple-element.124), channel_id=1, source_target_pairs={{0,2},{1,3},{2,0},{3,1},{4,6},{5,7},{6,4},{7,5},{8,10},{9,11},{10,... | collective-permute-start | bytes 1572872 | tf_op jit(solution)/shard_map/ppermute | solution.py:73
  486.0 64.2 %collective-permute-start.47 = (bf16[16,256,128]{2,1,0:T(8,128)(2,1)}, bf16[16,256,128]{2,1,0:T(8,128)(2,1)}, u32[]{:S(2)}, u32[]{:S(2)}) collective-permute-start(bf16[16,256,128]{2,1,0:T(8,128)(2,1)} %get-tuple-element.89), channel_id=1, source_target_pairs={{0,1},{1,0},{2,3},{3,2},{4,5},{5,4},{6,7},{7,6},{8,9},{9,8},{10,11... | collective-permute-start | bytes 3145736 | tf_op jit(solution)/shard_map/ppermute | solution.py:73
  502.1 86.1 %collective-permute-start.41 = (bf16[16,256,128]{2,1,0:T(8,128)(2,1)}, bf16[16,256,128]{2,1,0:T(8,128)(2,1)}, u32[]{:S(2)}, u32[]{:S(2)}) collective-permute-start(bf16[16,256,128]{2,1,0:T(8,128)(2,1)} %get-tuple-element.91), channel_id=1, source_target_pairs={{0,1},{1,0},{2,3},{3,2},{4,5},{5,4},{6,7},{7,6},{8,9},{9,8},{10,11... | collective-permute-start | bytes 3145736 | tf_op jit(solution)/shard_map/ppermute | solution.py:73
  524.6 107.8 %collective-permute-start.35 = (bf16[16,256,128]{2,1,0:T(8,128)(2,1)}, bf16[16,256,128]{2,1,0:T(8,128)(2,1)}, u32[]{:S(2)}, u32[]{:S(2)}) collective-permute-start(bf16[16,256,128]{2,1,0:T(8,128)(2,1)} %get-tuple-element.93), channel_id=1, source_target_pairs={{0,1},{1,0},{2,3},{3,2},{4,5},{5,4},{6,7},{7,6},{8,9},{9,8},{10,11... | collective-permute-start | bytes 3145736 | tf_op jit(solution)/shard_map/ppermute | solution.py:73
  544.0 129.1 %collective-permute-start.29 = (bf16[16,256,128]{2,1,0:T(8,128)(2,1)}, bf16[16,256,128]{2,1,0:T(8,128)(2,1)}, u32[]{:S(2)}, u32[]{:S(2)}) collective-permute-start(bf16[16,256,128]{2,1,0:T(8,128)(2,1)} %get-tuple-element.95), channel_id=1, source_target_pairs={{0,1},{1,0},{2,3},{3,2},{4,5},{5,4},{6,7},{7,6},{8,9},{9,8},{10,11... | collective-permute-start | bytes 3145736 | tf_op jit(solution)/shard_map/ppermute | solution.py:73
  (73 other events, 1167.2 us)
Sparse Core Ops, SparseCore 0:
  11.5 85.5 all-gather.4
  100.5 77.8 all-gather.6
  348.6 133.9 all-reduce.4
  484.8 155.3 reduce-scatter.4
  642.3 147.1 reduce-scatter.2

commit v2 on v1

v2 whole, which is shorter than its diff:
```python
import functools
import math

import jax
import jax.numpy as jnp
from jax import lax
from jax.experimental import pallas as pl
from jax.experimental.pallas import tpu as pltpu
from jax.sharding import PartitionSpec as P

mu_rate = 0.5
avg_decay = 0.5
task_weights = (1.0, 0.6, 0.8, 0.4, 1.2)
rates = (5000000.0, 12000.0, 3500.0, 1000.0, 370.0, 200.0)
both = ("dp", "mp")
lanes = 128
group = 32
window = 8
batch = 4
flag_bit = 20
f32, bf16, i32 = jnp.float32, jnp.bfloat16, jnp.int32
vmem_limit = 58 * 2**20


def bits_of(size):
    return int(size).bit_length() - 1


def cost(microseconds):
    return pl.CostEstimate(flops=int(microseconds * 1.1e9), bytes_accessed=int(microseconds * 3.0e6), transcendentals=0)


def params(limit=vmem_limit):
    return pltpu.CompilerParams(vmem_limit_bytes=limit)


def gelu_pair(h):
    scale = math.sqrt(2.0 / math.pi)
    square = h * h
    t = jnp.tanh(scale * h * (1.0 + 0.044715 * square))
    half = 0.5 * (1.0 + t)
    slope = half + 0.5 * h * (1.0 - t * t) * scale * (1.0 + 3.0 * 0.044715 * square)
    return h * half, slope


def nesterov(weight, moment, average, grad, rate):
    moment_new = mu_rate * moment + grad
    weight_new = weight - rate * (grad + mu_rate * moment_new)
    average_new = avg_decay * average + (1.0 - avg_decay) * weight_new
    return (weight_new, moment_new, average_new)


class Ring:
    def __init__(self, n_data, n_model):
        self.count = n_data * n_model
        tall = n_model // 2
        self.stages = (
            (0, 1),
            tuple(x * n_model + y * 2 for x in range(2) for y in range(tall)),
            tuple(z * 2 * n_model for z in range(n_data // 2)),
        )

    def offset_of(self, place):
        total = 0
        rest = place
        for stage in reversed(self.stages):
            digit = rest & (len(stage) - 1)
            rest = rest >> bits_of(len(stage))
            for bit in range(bits_of(len(stage))):
                total = total + ((digit >> bit) & 1) * stage[1 << bit]
        return total

    def device_at(self, me, place):
        return me ^ self.offset_of(place)

    def place_bits(self):
        places = {self.offset_of(place): place for place in range(self.count)}
        return [places[1 << bit] for bit in range(bits_of(self.count))]

    def swap(self, value, distance):
        return lax.ppermute(value, both, [(i, i ^ distance) for i in range(self.count)])

    def swap_pieces(self, stage, pieces):
        return [pieces[0]] + [self.swap(p, d) for p, d in zip(pieces[1:], self.stages[stage][1:])]

    def spread(self, stage, value):
        return [value] + [self.swap(value, d) for d in self.stages[stage][1:]]


def place_in(bits, offset):
    total = 0
    for bit, value in enumerate(bits):
        total = total + ((offset >> bit) & 1) * value
    return total


def sum_kernel(parts_in, parts_out, dtype, *refs):
    ins, outs = refs[:parts_in], refs[len(refs) - parts_out :]
    for k, out in enumerate(outs):
        total = ins[0][k].astype(f32)
        for ref in ins[1:]:
            total = total + ref[k].astype(f32)
        out[...] = total.astype(dtype)


def sum_pieces(parts, count, dtype, steps, after=(), name="sum"):
    length = parts[0].shape[0] // count
    rest = parts[0].shape[1:]
    fold = rest[:-2]
    blocks = length
    for size in fold:
        blocks = blocks * size
    steps = min(steps, blocks)
    each = blocks // steps
    tile = rest[-2:]
    views = [v.reshape((count, blocks) + tile) for v in parts]
    outs = pl.pallas_call(
        functools.partial(sum_kernel, len(parts), count, dtype),
        grid=(steps,),
        out_shape=[jax.ShapeDtypeStruct((blocks,) + tile, dtype)] * count,
        in_specs=[pl.BlockSpec((count, each) + tile, lambda i: (0, i, 0, 0))] * len(parts)
        + [pl.BlockSpec(memory_space=pl.ANY)] * len(after),
        out_specs=[pl.BlockSpec((each,) + tile, lambda i: (i, 0, 0))] * count,
        compiler_params=params(),
        name=name,
    )(*views, *after)
    return [v.reshape((length,) + rest) for v in outs]


def join_kernel(count, *refs):
    out = refs[-1]
    at = 0
    for ref in refs[:count]:
        out[at : at + ref.shape[0]] = ref[...]
        at += ref.shape[0]


def join(parts, after=()):
    total = sum(v.shape[0] for v in parts)
    anywhere = pl.BlockSpec(memory_space=pl.ANY)
    return pl.pallas_call(
        functools.partial(join_kernel, len(parts)),
        out_shape=jax.ShapeDtypeStruct((total,) + parts[0].shape[1:], parts[0].dtype),
        in_specs=[vmem()] * len(parts) + [anywhere] * len(after),
        out_specs=vmem(),
        compiler_params=params(),
        name="join",
    )(*parts, *after)


def held_until(value, after):
    anywhere = pl.BlockSpec(memory_space=pl.ANY)
    return pl.pallas_call(
        lambda *refs: None,
        out_shape=jax.ShapeDtypeStruct(value.shape, value.dtype),
        in_specs=[anywhere] * (1 + len(after)),
        out_specs=anywhere,
        input_output_aliases={0: 0},
        name="hold",
    )(value, *after)


def bucket_kernel(pairs, cap_rows, starts, keys, out):
    owners = out.shape[0]
    lane = lax.broadcasted_iota(i32, (1, lanes), 1)
    body_rows = -(-(cap_rows + 1) // 8) * 8

    def one(o, carry):
        off = starts[o * pairs]
        row = lax.shift_right_logical(off, 7)
        shift = off & (lanes - 1)
        block = keys[pl.ds(row, body_rows), :]
        turned = pltpu.roll(block, (lanes - shift) & (lanes - 1), 1)
        merged = jnp.where(lane < lanes - shift, turned[:cap_rows], turned[1 : cap_rows + 1])
        out[o, 0:cap_rows, :] = merged
        head = jnp.zeros((1, lanes), i32)
        for p in range(pairs + 1):
            head = jnp.where(lane == p, starts[o * pairs + p] - off, head)
        out[o, cap_rows : cap_rows + 1, :] = head
        return carry

    lax.fori_loop(0, owners, one, 0)


def prep_kernel(row_bits, sample_bits, entries, rows_out, samples_out):
    e = entries[...]
    rows = e & ((1 << row_bits) - 1)
    lane = lax.broadcasted_iota(i32, e.shape, 1)
    place = lane & (window - 1)
    clash = jnp.zeros(e.shape, i32)
    for d in range(1, window):
        other = pltpu.roll(rows, lanes - d, 1)
        clash = jnp.where((other == rows) & (place < window - d), 1, clash)
    step = 1
    while step < group:
        clash = clash | pltpu.roll(clash, lanes - step, 1)
        step *= 2
    rows_out[...] = jnp.where((lane & (group - 1)) == 0, rows | (clash << flag_bit), rows)
    samples_out[...] = lax.shift_right_logical(e, row_bits) & ((1 << sample_bits) - 1)


def one_hot(samples_ref, row, base, low, high, per_device, width):
    count = width // lanes
    s = jnp.concatenate([samples_ref[pl.ds(row + c, 1), :] for c in range(count)], axis=1)
    k = lax.broadcasted_iota(i32, (1, width), 1) + base
    s = jnp.where((k >= low) & (k < high), s, -1).astype(f32).astype(bf16)
    place = lax.broadcasted_iota(i32, (per_device, width), 0).astype(f32).astype(bf16)
    return jnp.where(place == s, jnp.ones((), bf16), jnp.zeros((), bf16))


class Lists:
    def __init__(self, ring, me, rows, held, sems):
        self.ring, self.me, self.rows, self.held, self.sems = ring, me, rows, held, sems
        self.length = held.shape[0] // (2 * batch)
        self.batches = rows.shape[0] // self.length // batch

    def copies(self, n):
        slot = n & 1
        found = []
        for b in range(batch):
            sender = self.ring.device_at(self.me[0], n * batch + b)
            source = self.rows.at[pl.ds(pl.multiple_of(sender * self.length, 1024), self.length)]
            held = self.held.at[pl.ds(pl.multiple_of((slot * batch + b) * self.length, 1024), self.length)]
            found.append(pltpu.make_async_copy(source, held, self.sems.at[slot, b]))
        return found

    def start(self, n):
        for copy in self.copies(n):
            copy.start()

    def wait(self, n):
        for copy in self.copies(n):
            copy.wait()

    def run(self, step):
        self.start(0)

        def one(n, carry):
            @pl.when(n + 1 < self.batches)
            def _():
                self.start(n + 1)

            self.wait(n)
            step(n)
            return carry

        lax.fori_loop(0, self.batches, one, 0)

    def first(self, n, b, at):
        return ((n & 1) * batch + b) * self.length + at

    def entry(self, place):
        return self.held[place] & ((1 << flag_bit) - 1)

    def clash(self, place):
        return lax.shift_right_logical(self.held[place], flag_bit)


def gather_kernel(ring, first_pair, at, per_device, cap, me, bounds, rows, samples, table, *refs):
    keep, send, rows_f, stage, pooled, held, sems, out_sem = refs[-8:]
    step = pl.program_id(0)
    pair = first_pair + step
    rows_own = table.shape[2]
    width = min(256, cap)
    cap_rows = cap // lanes
    blocks = cap // width
    span = 256
    lane = lax.broadcasted_iota(i32, (span, lanes), 1)
    same = lax.broadcasted_iota(i32, (span, span), 0) == lax.broadcasted_iota(i32, (span, span), 1)
    unit = jnp.where(same, 1.0, 0.0).astype(bf16)

    def turn(c, carry):
        at = pl.multiple_of(c * span, span)
        t = table[0, :, pl.ds(at, span)].astype(bf16)
        t = lax.dot_general(unit, t, (((1,), (1,)), ((), ())), preferred_element_type=f32)
        rows_f[pl.ds(at, span), :] = jnp.where(lane < lanes // 2, t, 0.0)
        at_odd = pl.multiple_of(c * span + rows_own, span)
        rows_f[pl.ds(at_odd, span), :] = jnp.where(lane < lanes // 2, 0.0, t)
        return carry

    lax.fori_loop(0, rows_own // span, turn, 0, unroll=8)
    stage[...] = jnp.zeros(stage.shape, f32)
    lists = Lists(ring, me, rows, held, sems)

    def some(n):
        senders = [ring.device_at(me[0], n * batch + b) for b in range(batch)]
        lows = [bounds[s * 8 + pair] for s in senders]
        highs = [bounds[s * 8 + pair + 1] for s in senders]
        for b in range(batch):

            def fetch(i, c):
                at = pl.multiple_of(i * group, group)
                first = lists.first(n, b, at)
                for u in range(group):
                    r = held[first + u] if u else lists.entry(first)
                    stage[b, pl.ds(at + u, 1), :] = rows_f[pl.ds(r, 1), :]
                return c

            lax.fori_loop(lax.div(lows[b], group), lax.div(highs[b] + group - 1, group), fetch, 0)

        def term(b, i):
            block = jnp.minimum(i, blocks - 1)
            row = senders[b] * cap_rows + block * (width // lanes)
            hot = one_hot(samples, row, i * width, lows[b], highs[b], per_device, width)
            fetched = stage[b, pl.ds(pl.multiple_of(block * width, width), width), :].astype(bf16)
            return jnp.dot(hot, fetched, preferred_element_type=f32)

        shift = bits_of(width)
        begins = [lax.shift_right_logical(low, shift) for low in lows]
        def put(b, total):
            pooled[pl.ds(n * batch + b, 1)] = total.astype(bf16)[None]

        for b in range(batch):
            put(b, term(b, begins[b]) + term(b, begins[b] + 1))
        for b in range(batch):

            @pl.when(highs[b] > (begins[b] + 2) * width)
            def _():
                total = lax.fori_loop(
                    begins[b],
                    lax.shift_right_logical(highs[b] + width - 1, shift),
                    lambda i, t: t + term(b, i),
                    jnp.zeros((per_device, lanes), f32),
                )
                put(b, total)

    lists.run(some)
    half = keep.shape[0]
    copies = [
        pltpu.make_async_copy(pooled.at[pl.ds(i * half, half)], ref.at[:, at + step], out_sem.at[i])
        for i, ref in enumerate((keep, send))
    ]
    for copy in copies:
        copy.start()
    for copy in copies:
        copy.wait()


def scatter_kernel(
    ring, pair, rows_at, per_device, cap, me, bounds, rows, samples, own, other, w_in, m_in, a_in, *refs
):
    w_out, m_out, a_out, sums, stage, grads, w_buf, m_buf, a_buf, held, sems, grad_sem, in_sem, out_sem = refs[-14:]
    blocks_each = own.shape[0]
    arrivals = [
        pltpu.make_async_copy(ref.at[:, pl.ds(rows_at, per_device)], grads.at[pl.ds(i * blocks_each, blocks_each)], grad_sem.at[i])
        for i, ref in enumerate((own, other))
    ]
    for arrival in arrivals:
        arrival.start()
    rows_own = w_in.shape[2]
    width = min(256, cap)
    cap_rows = cap // lanes
    blocks = cap // width
    sources = (w_in, m_in, a_in)
    targets = (w_out, m_out, a_out)
    buffers = (w_buf, m_buf, a_buf)
    sums[...] = jnp.zeros(sums.shape, f32)
    lists = Lists(ring, me, rows, held, sems)
    for arrival in arrivals:
        arrival.wait()
    for i in range(3):
        pltpu.make_async_copy(sources[i].at[pair], buffers[i], in_sem.at[i]).start()

    def some(n):
        senders = [ring.device_at(me[0], n * batch + b) for b in range(batch)]
        lows = [bounds[s * 8 + pair] for s in senders]
        highs = [bounds[s * 8 + pair + 1] for s in senders]

        def spread(b, i):
            block = jnp.minimum(i, blocks - 1)
            row = senders[b] * cap_rows + block * (width // lanes)
            hot = one_hot(samples, row, block * width, lows[b], highs[b], per_device, width)
            mine = grads[n * batch + b]
            stage[b, pl.ds(pl.multiple_of(block * width, width), width), :] = lax.dot_general(
                hot, mine, (((0,), (0,)), ((), ())), preferred_element_type=f32
            )

        shift = bits_of(width)
        begins = [lax.shift_right_logical(low, shift) for low in lows]
        for b in range(batch):
            spread(b, begins[b])
            spread(b, begins[b] + 1)
        for b in range(batch):

            @pl.when(highs[b] > (begins[b] + 2) * width)
            def _():
                def more(i, c):
                    spread(b, i)
                    return c

                lax.fori_loop(begins[b] + 2, lax.shift_right_logical(highs[b] + width - 1, shift), more, 0)

        for b in range(batch):

            def add(i, c):
                at = pl.multiple_of(i * group, group)
                first = lists.first(n, b, at)

                def apart():
                    for start in range(0, group, window):
                        places = [held[first + u] if u else lists.entry(first) for u in range(start, start + window)]
                        olds = [sums[pl.ds(r, 1), :] for r in places]
                        news = [stage[b, pl.ds(at + start + u, 1), :] for u in range(window)]
                        for r, old, new in zip(places, olds, news):
                            sums[pl.ds(r, 1), :] = old + new

                def in_turn():
                    def single(u, inner):
                        r = lists.entry(first + u)
                        sums[pl.ds(r, 1), :] = sums[pl.ds(r, 1), :] + stage[b, pl.ds(at + u, 1), :]
                        return inner

                    lax.fori_loop(0, group, single, 0)

                lax.cond(lists.clash(first) == 0, apart, in_turn)
                return c

            lax.fori_loop(lax.div(lows[b], group), lax.div(highs[b] + group - 1, group), add, 0)

    lists.run(some)
    for i in range(3):
        pltpu.make_async_copy(sources[i].at[pair], buffers[i], in_sem.at[i]).wait()
    chunks = out_sem.shape[0] // 3
    chunk = rows_own // chunks
    span = min(256, chunk)
    lane = lax.broadcasted_iota(i32, (span, lanes), 1)

    def copies(n):
        part = pl.ds(n * chunk, chunk)
        return [
            pltpu.make_async_copy(buffers[i].at[:, part], targets[i].at[pair, :, part], out_sem.at[n * 3 + i])
            for i in range(3)
        ]

    for n in range(chunks):

        def update(c, carry):
            at = pl.multiple_of(n * chunk + c * span, span)
            even = sums[pl.ds(at, span), :]
            odd = sums[pl.ds(pl.multiple_of(at + rows_own, span), span), :]
            grad = jnp.where(lane < lanes // 2, even, odd).T
            part = (slice(None), pl.ds(at, span))
            new = nesterov(w_buf[part], m_buf[part], a_buf[part], grad, rates[0])
            w_buf[part] = new[0]
            m_buf[part] = new[1]
            a_buf[part] = new[2]
            return carry

        lax.fori_loop(0, chunk // span, update, 0)
        for copy in copies(n):
            copy.start()
    for n in range(chunks):
        for copy in copies(n):
            copy.wait()


rows_first = (((0,), (0,)), ((), ()))
last_last = (((1,), (1,)), ((), ()))


def experts_forward(x_ref, weight_ref, y_ref, act_ref, slope_ref):
    x = x_ref[...]
    total = None
    for m in range(weight_ref.shape[1]):
        w_in, w_out = (weight_ref[:, m, i, 0].reshape(-1, weight_ref.shape[-1]) for i in range(2))
        act, slope = gelu_pair(jnp.dot(x, w_in, preferred_element_type=f32))
        act = act.astype(bf16)
        act_ref[0, m] = act
        slope_ref[0, m] = slope.astype(bf16)
        term = lax.dot_general(act, w_out, last_last, preferred_element_type=f32)
        total = term if total is None else total + term
    y_ref[0] = total


def experts_back_rows(pairs, d_ref, weight_ref, slope_ref, dxg_ref, inv_ref, d_hidden_ref, *refs):
    grads, dx = refs[:pairs], refs[pairs]
    d_out = d_ref[0]
    total = None
    for m in range(weight_ref.shape[1]):
        w_in, w_out = (weight_ref[:, m, i, 0].reshape(-1, weight_ref.shape[-1]) for i in range(2))
        d_act = jnp.dot(d_out, w_out, preferred_element_type=f32)
        d_hidden = (d_act * slope_ref[0, m].astype(f32)).astype(bf16)
        d_hidden_ref[0, m] = d_hidden
        term = lax.dot_general(d_hidden, w_in, last_last, preferred_element_type=f32)
        total = term if total is None else total + term

    @pl.when(pl.program_id(0) == 0)
    def _():
        dx[...] = dxg_ref[...] + total

    @pl.when(pl.program_id(0) != 0)
    def _():
        dx[...] += total

    @pl.when(pl.program_id(0) == pl.num_programs(0) - 1)
    def _():
        for p in range(pairs):
            part = (slice(None), slice(p * lanes, (p + 1) * lanes))
            grads[p][...] = (dx[part] * inv_ref[part]).astype(bf16)


def experts_back_weights(n_model, lhs_ref, rows_ref, *refs):
    dw_ref = refs[-1]
    devices, _, f_own, _ = dw_ref.shape
    lhs = lhs_ref[0]
    for m in range(n_model):
        out = jnp.dot(lhs, rows_ref[0, m], preferred_element_type=f32).astype(bf16)
        for d in range(devices // n_model):
            dw_ref[d * n_model + m, 0] = out[d * f_own : (d + 1) * f_own]


def experts_back_placed(bits, n_model, me, lhs_ref, rows_ref, *refs):
    keep, send = refs[-2:]
    half, _, f_own, h_own = keep.shape
    model = me[0] & (n_model - 1)
    data = me[0] ^ model
    bits = [0] + bits[1:]
    lhs = lhs_ref[0]
    for beside in range(n_model):
        out = jnp.dot(lhs, rows_ref[0, pl.ds(model ^ beside, 1)][0], preferred_element_type=f32).astype(bf16)
        to = send if beside & 1 else keep
        for d in range(2 * half // n_model):
            place = place_in(bits, (data ^ (d * n_model)) | (beside & (n_model - 2)))
            to[pl.ds(place, 1), 0] = out[d * f_own : (d + 1) * f_own][None]


def head_kernel(
    sample_total, x_ref, y_ref, gate_ref, tower_ref, v_ref, label_ref,
    d_expert_ref, d_expert_t_ref, dxg_ref, d_tower_ref, d_gate_ref, small_ref, probs, mixed, d_mixed, d_gate, inner,
):
    experts, rows, features = y_ref.shape
    tasks = tower_ref.shape[0]
    x = x_ref[...]
    gate = gate_ref[...]
    logits = jnp.dot(x, gate, preferred_element_type=f32)
    task_of = lax.shift_right_logical(lax.broadcasted_iota(i32, (1, lanes), 1), bits_of(experts))

    def by_task(fold, value, fill):
        total = jnp.zeros(value.shape, f32)
        for k in range(tasks):
            found = fold(jnp.where(task_of == k, value, fill), axis=1, keepdims=True)
            total = jnp.where(task_of == k, found, total)
        return total

    used = task_of < tasks
    raised = jnp.where(used, jnp.exp(logits - by_task(jnp.max, logits, -jnp.inf)), 0.0)
    probs[...] = raised / jnp.where(used, by_task(jnp.sum, raised, 0.0), 1.0)
    span = 16
    parts = 2
    wide = features // parts

    def mix(r, carry):
        part = pl.ds(pl.multiple_of(r * span, span), span)
        p = probs[part, :]
        for h in range(parts):
            across = slice(h * wide, (h + 1) * wide)
            totals = [None] * tasks
            for e in range(experts):
                y = y_ref[e, part, across]
                for k in range(tasks):
                    c = k * experts + e
                    more = p[:, c : c + 1] * y
                    totals[k] = more if e == 0 else totals[k] + more
            for k in range(tasks):
                mixed[k, part, across] = totals[k].astype(bf16)
        return carry

    lax.fori_loop(0, rows // span, mix, 0)
    loss = jnp.zeros((1, 1), f32)
    vectors = []
    for k in range(tasks):
        tower = tower_ref[k]
        act, slope = gelu_pair(jnp.dot(mixed[k], tower, preferred_element_type=f32))
        v = v_ref[k : k + 1, :]
        logit = jnp.sum(act * v, axis=1, keepdims=True)
        label = label_ref[:, k : k + 1]
        weighting = task_weights[k] * label_ref[:, tasks + k : tasks + k + 1]
        small_exp = jnp.exp(-jnp.abs(logit))
        softplus = jnp.maximum(logit, 0.0) + jnp.log1p(small_exp)
        loss = loss + jnp.sum(weighting * (softplus - label * logit), axis=0, keepdims=True)
        sigmoid = jnp.where(logit >= 0.0, 1.0, small_exp) / (1.0 + small_exp)
        d_logit = weighting * (sigmoid - label) / sample_total
        vectors.append(jnp.sum(d_logit * act, axis=0, keepdims=True))
        d_pre = (d_logit * v * slope).astype(bf16)
        d_mixed[k] = lax.dot_general(d_pre, tower, last_last, preferred_element_type=f32)
        d_tower_ref[k] = lax.dot_general(mixed[k], d_pre, rows_first, preferred_element_type=f32).astype(bf16)
    lane = lax.broadcasted_iota(i32, (span, lanes), 1)
    ones = jnp.ones((lanes, lanes), bf16)

    def back(r, carry):
        part = pl.ds(pl.multiple_of(r * span, span), span)
        p = probs[part, :]
        for e in range(experts):
            y = y_ref[e, part, :]
            total = None
            for k in range(tasks):
                c = k * experts + e
                d = d_mixed[k, part, :]
                product = d * y
                narrow = product[:, :lanes]
                for t in range(1, features // lanes):
                    narrow = narrow + product[:, t * lanes : (t + 1) * lanes]
                coarse = narrow.astype(bf16)
                inner[0, c * span : (c + 1) * span, :] = coarse
                inner[1, c * span : (c + 1) * span, :] = (narrow - coarse.astype(f32)).astype(bf16)
                more = p[:, c : c + 1] * d
                total = more if k == 0 else total + more
            d_expert_ref[e, part, :] = total.astype(bf16)
        row_sums = jnp.dot(inner[0], ones, preferred_element_type=f32)
        row_sums = row_sums + jnp.dot(inner[1], ones, preferred_element_type=f32)
        d_probs = jnp.zeros((span, lanes), f32)
        for c in range(tasks * experts):
            d_probs = jnp.where(lane == c, row_sums[c * span : (c + 1) * span], d_probs)
        d_gate[part, :] = (p * (d_probs - by_task(jnp.sum, p * d_probs, 0.0))).astype(bf16)
        return carry

    lax.fori_loop(0, rows // span, back, 0)
    for e in range(experts):
        d_expert_t_ref[e] = d_expert_ref[e].T
    dxg_ref[...] = lax.dot_general(d_gate[...], gate, last_last, preferred_element_type=f32)
    d_gate_ref[...] = lax.dot_general(x, d_gate[...], rows_first, preferred_element_type=f32).astype(bf16)
    line = lax.broadcasted_iota(i32, (8, lanes), 0)
    tile = jnp.where(line == tasks, loss, 0.0)
    for k in range(tasks):
        tile = jnp.where(line == k, vectors[k], tile)
    pieces = []
    for _ in range(4):
        piece = tile.astype(bf16)
        pieces.append(piece)
        tile = tile - piece.astype(f32)
    small_ref[...] = jnp.concatenate(pieces, axis=0)


def smem():
    return pl.BlockSpec(memory_space=pltpu.SMEM)


def vmem():
    return pl.BlockSpec(memory_space=pltpu.VMEM)


def body(
    row_ids, bag_counts, labels, label_mask, tables, table_mom, table_avg, w_in, w_in_mom, w_in_avg,
    w_out, w_out_mom, w_out_avg, gate_w, gate_mom, gate_avg, tower_w, tower_w_mom, tower_w_avg,
    tower_v, tower_v_mom, tower_v_avg,
):
    n_model = lax.axis_size("mp")
    n_data = lax.axis_size("dp")
    devices = n_data * n_model
    ring = Ring(n_data, n_model)
    mp_rank = lax.axis_index("mp")
    me = (lax.axis_index("dp") * n_model + mp_rank).astype(i32).reshape(1)
    per_group, table_count, bag_size = row_ids.shape
    per_device = per_group // n_model
    rows_own = tables.shape[1]
    emb_width = tables.shape[2]
    features = table_count * emb_width
    pairs = features // lanes
    sample_total = float(per_group * n_data)
    slot_total = per_device * table_count * bag_size
    cap = 2 * slot_total // devices
    cap_rows = cap // lanes

    w_out_t, w_out_mom_t, w_out_avg_t = (v.transpose(0, 2, 1) for v in (w_out, w_out_mom, w_out_avg))
    experts, f_own, h_own = w_in.shape
    weights = jnp.stack([w_in, w_out_t]).astype(bf16)
    weights = lax.all_gather(weights, both, axis=0).reshape(n_data, n_model, 2, experts, f_own, h_own)

    row_bits = bits_of(rows_own) + 1
    sample_bits = bits_of(per_device)
    start = mp_rank * per_device
    ids = lax.dynamic_slice_in_dim(row_ids.transpose(1, 2, 0), start, per_device, 2)
    counts = lax.dynamic_slice_in_dim(bag_counts.T, start, per_device, 1)
    live = lax.broadcasted_iota(i32, ids.shape, 1) < counts[:, None, :]
    table_of = lax.broadcasted_iota(i32, ids.shape, 0)
    bucket = lax.shift_right_logical(ids, row_bits - 1) * pairs + lax.shift_right_logical(table_of, 1)
    key = (bucket << sample_bits) | lax.broadcasted_iota(i32, ids.shape, 2)
    key = (((key << 1) | (table_of & 1)) << (row_bits - 1)) | (ids & (rows_own - 1))
    key = jnp.where(live, key, 1 << 30).reshape(-1)
    ordered = lax.sort(key)
    bucket_sorted = lax.shift_right_logical(ordered, row_bits + sample_bits)
    starts = jnp.sum(
        (bucket_sorted[None, :] < jnp.arange(devices * pairs + 1, dtype=i32)[:, None]).astype(i32), axis=1
    )
    padded = jnp.concatenate([ordered.reshape(-1, lanes), jnp.zeros((cap_rows + 8, lanes), i32)], axis=0)
    out_rows = -(-(cap_rows + 1) // 8) * 8
    outgoing = pl.pallas_call(
        functools.partial(bucket_kernel, pairs, cap_rows),
        out_shape=jax.ShapeDtypeStruct((devices, out_rows, lanes), i32),
        in_specs=[smem(), vmem()],
        out_specs=vmem(),
        name="bucket",
    )(starts, padded)
    received = lax.all_to_all(outgoing, both, split_axis=0, concat_axis=0, tiled=True)
    bounds = received[:, cap_rows, :8].reshape(-1)
    entries = received[:, :cap_rows].reshape(devices * cap_rows, lanes)
    entry_shape = jax.ShapeDtypeStruct(entries.shape, i32)
    rows, samples = pl.pallas_call(
        functools.partial(prep_kernel, row_bits, sample_bits),
        out_shape=(entry_shape, entry_shape),
        in_specs=[vmem()],
        out_specs=(vmem(), vmem()),
        name="prep",
    )(entries)
    length = max(cap, 1024)
    rows = jnp.pad(rows.reshape(devices, cap), ((0, 0), (0, length - cap))).reshape(-1)
    hbm = pl.BlockSpec(memory_space=pl.ANY)
    list_scratch = [pltpu.SMEM((2 * batch * length,), i32), pltpu.SemaphoreType.DMA((2, batch))]

    paired = tuple(
        v.transpose(0, 2, 1).reshape(pairs, lanes, rows_own) for v in (tables, table_mom, table_avg)
    )
    half = devices // 2
    half_shape = jax.ShapeDtypeStruct((half, per_device, lanes), bf16)

    def gather(first_pair, count, at, total, olds, after):
        out_shape = jax.ShapeDtypeStruct((half, total, per_device, lanes), bf16)
        return pl.pallas_call(
            functools.partial(gather_kernel, ring, first_pair, at, per_device, cap),
            grid=(count,),
            out_shape=(out_shape, out_shape),
            in_specs=[
                smem(), smem(), hbm, vmem(),
                pl.BlockSpec((1, lanes, rows_own), lambda i: (first_pair + i, 0, 0)),
            ] + [hbm] * (len(olds) + len(after)),
            out_specs=(hbm, hbm),
            scratch_shapes=[
                pltpu.VMEM((2 * rows_own, lanes), f32),
                pltpu.VMEM((batch, cap, lanes), f32),
                pltpu.VMEM((devices, per_device, lanes), bf16),
            ] + list_scratch + [pltpu.SemaphoreType.DMA((2,))],
            input_output_aliases={5: 0, 6: 1} if olds else {},
            compiler_params=params(),
            cost_estimate=cost(16 * count),
            name="gather",
        )(me, bounds, rows, samples, paired[0], *olds, *after)

    plane, line = len(ring.stages[1]), len(ring.stages[2])
    each = half // plane

    def core_sums(keep, send, steps, after=(), name="sum_core"):
        return sum_pieces([keep, ring.swap(send, 1)], plane, bf16, steps, after, name)

    def plane_sums(pieces, steps, after=(), name="sum_plane"):
        return sum_pieces(ring.swap_pieces(1, pieces), line, bf16, steps, after, name)

    def line_sum(pieces):
        total = None
        for piece in ring.swap_pieces(2, pieces):
            total = piece.astype(f32) if total is None else total + piece.astype(f32)
        return total

    early = pairs // 2
    rest = pairs - early
    cored_early = core_sums(*gather(0, early, 0, early, (), ()), 2)
    late = gather(early, rest - 1, 0, rest, (), ())
    late = gather(pairs - 1, 1, rest - 1, rest, late, (cored_early[0],))
    planed_early = plane_sums(cored_early, 1)
    cored_late = core_sums(late[0], held_until(late[1], (planed_early[0],)), 2)
    planed_late = plane_sums(cored_late, 1)
    pooled = jnp.concatenate([line_sum(planed_early)[0], line_sum(planed_late)[0]], axis=0)
    inverse = jnp.repeat(1.0 / counts.T.astype(f32), emb_width, axis=1)
    x = (pooled.transpose(1, 0, 2).reshape(per_device, features) * inverse).astype(bf16)

    hidden_shape = jax.ShapeDtypeStruct((experts, n_model, per_device, h_own), bf16)
    weight_spec = pl.BlockSpec((n_data, n_model, 2, 1, f_own, h_own), lambda e: (0, 0, 0, e, 0, 0))
    hidden_spec = pl.BlockSpec((1, n_model, per_device, h_own), lambda e: (e, 0, 0, 0))
    expert_spec = pl.BlockSpec((1, per_device, features), lambda e: (e, 0, 0))
    whole_spec = pl.BlockSpec((per_device, features), lambda e: (0, 0))
    y, act, slope = pl.pallas_call(
        experts_forward,
        grid=(experts,),
        out_shape=(jax.ShapeDtypeStruct((experts, per_device, features), f32), hidden_shape, hidden_shape),
        in_specs=[whole_spec, weight_spec],
        out_specs=(expert_spec, hidden_spec, hidden_spec),
        compiler_params=params(),
        cost_estimate=cost(16),
        name="experts_forward",
    )(x, weights)
    tasks, _, tower_width = tower_w.shape
    spare = lanes - tasks * experts
    gate_low = jnp.pad(gate_w.transpose(1, 0, 2).reshape(features, tasks * experts), ((0, 0), (0, spare))).astype(bf16)
    label_rows = lax.dynamic_slice_in_dim(labels, start, per_device, 0)
    mask_rows = lax.dynamic_slice_in_dim(label_mask, start, per_device, 0)
    marks = jnp.concatenate([label_rows, mask_rows], axis=1).astype(f32)
    d_expert, d_expert_t, d_x_gate, d_tower_part, d_gate_part, tiny = pl.pallas_call(
        functools.partial(head_kernel, sample_total),
        out_shape=(
            jax.ShapeDtypeStruct((experts, per_device, features), bf16),
            jax.ShapeDtypeStruct((experts, features, per_device), bf16),
            jax.ShapeDtypeStruct((per_device, features), f32),
            jax.ShapeDtypeStruct(tower_w.shape, bf16),
            jax.ShapeDtypeStruct((features, lanes), bf16),
            jax.ShapeDtypeStruct((32, lanes), bf16),
        ),
        in_specs=[vmem()] * 6,
        out_specs=(vmem(),) * 6,
        scratch_shapes=[
            pltpu.VMEM((per_device, lanes), f32),
            pltpu.VMEM((tasks, per_device, features), bf16),
            pltpu.VMEM((tasks, per_device, features), f32),
            pltpu.VMEM((per_device, lanes), bf16),
            pltpu.VMEM((2, 16 * tasks * experts, lanes), bf16),
        ],
        compiler_params=params(),
        cost_estimate=cost(12),
        name="towers",
    )(x, y, gate_low, tower_w.astype(bf16), tower_v, marks)
    grads_shape = jax.ShapeDtypeStruct((per_device, lanes), bf16)
    d_hidden, *grads = pl.pallas_call(
        functools.partial(experts_back_rows, pairs),
        grid=(experts,),
        out_shape=(hidden_shape,) + (grads_shape,) * pairs,
        in_specs=[expert_spec, weight_spec, hidden_spec, whole_spec, whole_spec],
        out_specs=(hidden_spec,) + (pl.BlockSpec((per_device, lanes), lambda e: (0, 0)),) * pairs,
        scratch_shapes=[pltpu.VMEM((per_device, features), f32)],
        compiler_params=params(),
        cost_estimate=cost(14),
        name="experts_back_rows",
    )(d_expert, weights, slope, d_x_gate, inverse)
    grads = jnp.concatenate([grads[0], tiny] + grads[1:], axis=0)[None]

    lhs_spec = [
        pl.BlockSpec((1, features, per_device), lambda e, single=single: (0 if single else e, 0, 0))
        for single in (False, True)
    ]
    rows_spec = pl.BlockSpec((1, n_model, per_device, h_own), lambda e: (e, 0, 0, 0))
    half_weights = jax.ShapeDtypeStruct((half, experts, f_own, h_own), bf16)
    half_spec = pl.BlockSpec((half, 1, f_own, h_own), lambda e: (0, e, 0, 0))

    paired_shape = jax.ShapeDtypeStruct(paired[0].shape, f32)
    chunks = 4

    def scatter(pair, at, own, other, olds, after):
        in_specs = [smem(), smem(), hbm, vmem()] + [hbm] * (5 + len(olds) + len(after))
        return pl.pallas_call(
            functools.partial(scatter_kernel, ring, pair, at, per_device, cap),
            out_shape=(paired_shape,) * 3,
            in_specs=in_specs,
            out_specs=(hbm, hbm, hbm),
            scratch_shapes=[
                pltpu.VMEM((2 * rows_own, lanes), f32),
                pltpu.VMEM((batch, cap, lanes), f32),
                pltpu.VMEM((devices, per_device, lanes), bf16),
                pltpu.VMEM((lanes, rows_own), f32),
                pltpu.VMEM((lanes, rows_own), f32),
                pltpu.VMEM((lanes, rows_own), f32),
                *list_scratch,
                pltpu.SemaphoreType.DMA((2,)),
                pltpu.SemaphoreType.DMA((3,)),
                pltpu.SemaphoreType.DMA((3 * chunks,)),
            ],
            input_output_aliases={9: 0, 10: 1, 11: 2} if olds else {},
            compiler_params=params(),
            cost_estimate=cost(26),
            name="scatter",
        )(me, bounds, rows, samples, own, other, *paired, *olds, *after)

    small_rows = tasks * features + features
    small = jnp.concatenate([d_tower_part.reshape(-1, lanes), d_gate_part], axis=0).reshape(2, 1, small_rows // 2, lanes)
    side = me[0] & 1
    give = lax.dynamic_index_in_dim(small, 1 - side, 0, keepdims=False)
    take = lax.dynamic_index_in_dim(small, side, 0, keepdims=False)
    distances = [1 << bit for bit in range(bits_of(devices))]

    def add_small(after):
        got = ring.swap(give, distances.pop(0)) if distances else None
        return take if got is None else sum_pieces([take, got], 1, bf16, 1, after, "sum_small")[0]

    dw_out = pl.pallas_call(
        functools.partial(experts_back_weights, n_model),
        grid=(experts,),
        out_shape=jax.ShapeDtypeStruct((devices, experts, f_own, h_own), bf16),
        in_specs=[lhs_spec[0], rows_spec],
        out_specs=pl.BlockSpec((devices, 1, f_own, h_own), lambda e: (0, e, 0, 0)),
        compiler_params=params(),
        cost_estimate=cost(9),
        name="experts_back_out",
    )(d_expert_t, act)
    lined = join(ring.spread(2, grads), (dw_out,))
    give = take = add_small((dw_out,))
    d_w_out = lax.psum_scatter(dw_out, both, scatter_dimension=0, tiled=True)[0].astype(f32)
    keep, send = pl.pallas_call(
        functools.partial(experts_back_placed, ring.place_bits(), n_model),
        grid=(experts,),
        out_shape=(half_weights, half_weights),
        in_specs=[smem(), lhs_spec[1], rows_spec, hbm, hbm],
        out_specs=(half_spec, half_spec),
        compiler_params=params(),
        cost_estimate=cost(9),
        name="experts_back_in",
    )(me, x.T[None], d_hidden, lined, dw_out)
    give = take = add_small((keep,))
    with_tiny = per_device + tiny.shape[0]
    edges = (0, with_tiny, with_tiny + per_device, lined.shape[1])
    spread = [ring.spread(1, lined[:, low:high]) for low, high in zip(edges, edges[1:])]
    cored = core_sums(keep, send, 8, (give,), "sum_core_w")
    own = join(spread[0], (cored[0],))
    other = ring.swap(own, 1)
    give = take = add_small((own,))
    tiny_sum = jnp.sum(jnp.concatenate([own[:, per_device:], other[:, per_device:]]).astype(f32), axis=0)
    table_outs = scatter(0, 0, own, other, (), (give,))
    own = join(spread[1], (table_outs[0],))
    other = ring.swap(own, 1)
    give = take = add_small((own,))
    table_outs = scatter(1, 0, own, other, table_outs, (give,))
    own = join(spread[2], (table_outs[0],))
    other = ring.swap(own, 1)
    while distances:
        give = take = add_small((own,))
    table_outs = scatter(2, 0, own, other, table_outs, (give,))
    for pair in range(3, pairs):
        after = ()
        if pair == pairs - 1:
            planed = plane_sums(cored, 4, (table_outs[0],), "sum_plane_w")
            after = (planed[0],)
        table_outs = scatter(pair, (pair - 2) * per_device, own, other, table_outs, after)
    got = ring.swap(take, 1)
    small = jnp.concatenate([jnp.where(side == 0, take, got), jnp.where(side == 0, got, take)]).astype(f32)
    small = small.reshape(small_rows, lanes)
    d_tower_w = small[: tasks * features].reshape(tower_w.shape)
    d_gate_w = small[tasks * features :, : tasks * experts]
    d_gate_w = d_gate_w.reshape(features, tasks, experts).transpose(1, 0, 2)
    d_w_in = line_sum(planed)[0]
    tiny_sum = jnp.sum(tiny_sum.reshape(4, 8, lanes), axis=0)
    d_tower_v, loss_sum = tiny_sum[:tasks], tiny_sum[tasks, 0]
    table_new = tuple(v.reshape(table_count, emb_width, rows_own).transpose(0, 2, 1) for v in table_outs)
    w_in_new = nesterov(w_in, w_in_mom, w_in_avg, d_w_in, rates[1])
    w_out_new = nesterov(w_out_t, w_out_mom_t, w_out_avg_t, d_w_out, rates[2])
    w_out_new = tuple(v.transpose(0, 2, 1) for v in w_out_new)
    gate_new = nesterov(gate_w, gate_mom, gate_avg, d_gate_w, rates[3])
    tower_new = nesterov(tower_w, tower_w_mom, tower_w_avg, d_tower_w, rates[4])
    vector_new = nesterov(tower_v, tower_v_mom, tower_v_avg, d_tower_v, rates[5])
    return (loss_sum,) + table_new + w_in_new + w_out_new + gate_new + tower_new + vector_new


def solution(mesh):
    group_spec = P("dp", None)
    table_spec = P(None, both, None)
    placed = (
        (P("dp", None, None), group_spec, group_spec, group_spec)
        + (table_spec,) * 3
        + (P(None, "dp", "mp"),) * 3
        + (P(None, "mp", "dp"),) * 3
        + (P(),) * 9
    )
    return jax.shard_map(
        body,
        mesh=mesh,
        in_specs=placed,
        out_specs=(P(),)
        + (table_spec,) * 3
        + (P(None, "dp", "mp"),) * 3
        + (P(None, "mp", "dp"),) * 3
        + (P(),) * 9,
        check_vma=False,
    )
```

time: 810 us -> 573 us (0.71)
  the two profiles are of different devices: /device:TPU:0 before, /device:TPU:20 now
where the time goes in v2:
time: 573 us; the launch traced here: 562 us
  Pallas kernels  336 us (59%)
  waiting for transfers between devices  107 us (19%)
  starting transfers between devices  40.8 us (7%)
  other arithmetic  33 us (6%)
  local copies, waits for them, and re-layouts  31 us (5%)
  between operations  15.1 us (3%)
    pallas_call x4, Pallas kernels, scatter(): pl.pallas_call(functools.partial(scatter_kernel, ring, pair, at, per_devi...  136 us
    ppermute x42, waiting for transfers between devices, swap(): lax.ppermute(value, both, [(i, i ^ distance) for i in range(self.count)])  90 us
    pallas_call x3, Pallas kernels, gather(): pl.pallas_call(functools.partial(gather_kernel, ring, first_pair, at, per...  82.3 us
    ppermute x42, starting transfers between devices, swap(): lax.ppermute(value, both, [(i, i ^ distance) for i in range(self.count)])  34.9 us
    pallas_call x11, Pallas kernels, sum_pieces(): pl.pallas_call(functools.partial(sum_kernel, len(parts), count, dtype), g...  33.1 us
    unnamed x113, local copies, waits for them, and re-layouts  18.9 us
    pallas_call x1, Pallas kernels, body(): pl.pallas_call(functools.partial(head_kernel, sample_total), out_shape=(j...  18.1 us
    pallas_call x1, Pallas kernels, body(): pl.pallas_call(experts_forward, grid=(experts,), out_shape=(jax.ShapeDtyp...  16.6 us
  transfers between devices with their start and end apart: 45, of which 15 were waited for; matrix products, arithmetic and copies ran while one was open for 7% of the time, Pallas kernels for 49%

profile of v2, /device:TPU:20, one launch (start us, length us, event | category | flops | bytes accessed | tf_op | source)
XLA Modules:
  0.0 562.1 jit_solution(6331187966719600767)
XLA Ops:
  11.4 11.2 %sort.14 = (s32[32768]{0:T(1024)S(1)}, s32[32768]{0:T(1024)}) sort(s32[32768]{0:T(1024)S(1)} %bitcast.201, s32[32768]{0:T(1024)S(1)} %iota.33), dimensions={0}, to_apply=%region_0.1 | sort | flops 491520 | bytes 524288 | tf_op jit(solution)/shard_map/sort | solution.py:680
  30.4 5.9 %all-to-all-start = ((s32[32,24,128]{2,1,0:T(8,128)}), s32[32,24,128]{2,1,0:T(8,128)S(1)}, u32[]{:S(2)}, u32[]{:S(2)}) async-start(s32[32,24,128]{2,1,0:T(8,128)} %bucket.1), calls=%async_computation | async-start | bytes 786432 | tf_op jit(solution)/shard_map/all_to_all | solution.py:694
  36.4 16.5 %all-to-all-done = s32[32,24,128]{2,1,0:T(8,128)S(1)} async-done(((s32[32,24,128]{2,1,0:T(8,128)}), s32[32,24,128]{2,1,0:T(8,128)S(1)}, u32[]{:S(2)}, u32[]{:S(2)}) %all-to-all-start) | async-done | bytes 393248 | tf_op jit(solution)/shard_map/all_to_all | solution.py:694
  57.0 39.2 %gather.3 = (bf16[16,2,256,128]{3,2,1,0:T(8,128)(2,1)}, bf16[16,2,256,128]{3,2,1,0:T(8,128)(2,1)}) custom-call(s32[1]{0:T(128)} %bitcast.me, s32[256]{0:T(256)} %reshape_squeeze.3.bounds, s32[65536]{0:T(1024)} %bitcast.242, s32[512,128]{1,0:T(8,128)} %get-tuple-element.83.samples, f32[4,128,8192]{2,1,0:T(8,128)} %bitcast.216), custom_call_target="tpu_custom_call" | custom-call | flops 35200000000 | bytes 96000000 | tf_op jit(solution)/shard_map/gather/pallas_call | solution.py:718
  96.2 22.4 %gather.4 = (bf16[16,2,256,128]{3,2,1,0:T(8,128)(2,1)}, bf16[16,2,256,128]{3,2,1,0:T(8,128)(2,1)}) custom-call(s32[1]{0:T(128)} %bitcast.me, s32[256]{0:T(256)} %reshape_squeeze.3.bounds, s32[65536]{0:T(1024)} %bitcast.243, s32[512,128]{1,0:T(8,128)} %get-tuple-element.83.samples, f32[4,128,8192]{2,1,0:T(8,128)} %bitcast.217), custom_call_target="tpu_custom_call" | custom-call | flops 17600000000 | bytes 48000000 | tf_op jit(solution)/shard_map/gather/pallas_call | solution.py:718
  126.8 20.7 %gather.5 = (bf16[16,2,256,128]{3,2,1,0:T(8,128)(2,1)}, bf16[16,2,256,128]{3,2,1,0:T(8,128)(2,1)}) custom-call(s32[1]{0:T(128)} %bitcast.me, s32[256]{0:T(256)} %reshape_squeeze.3.bounds, s32[65536]{0:T(1024)} %bitcast.244, s32[512,128]{1,0:T(8,128)} %get-tuple-element.83.samples, ...), custom_call_target="tpu_custom_call", output_to_operand_aliasing={{0}: (5, {}), {1}: (6, {})} | custom-call | flops 17600000000 | bytes 48000000 | tf_op jit(solution)/shard_map/gather/pallas_call | solution.py:718
  165.1 9.8 %collective-permute-done.8.refs_1_ = bf16[4,2,256,128]{3,2,1,0:T(8,128)(2,1)S(1)} collective-permute-done((bf16[4,2,256,128]{3,2,1,0:T(8,128)(2,1)}, bf16[4,2,256,128]{3,2,1,0:T(8,128)(2,1)S(1)}, u32[]{:S(2)}, u32[]{:S(2)}) %collective-permute-start.8) | collective-permute-done | bytes 524320 | tf_op jit(solution)/shard_map/ppermute | solution.py:81
  178.5 8.9 %collective-permute-done.10.refs_3_ = bf16[4,2,256,128]{3,2,1,0:T(8,128)(2,1)S(1)} collective-permute-done((bf16[4,2,256,128]{3,2,1,0:T(8,128)(2,1)}, bf16[4,2,256,128]{3,2,1,0:T(8,128)(2,1)S(1)}, u32[]{:S(2)}, u32[]{:S(2)}) %collective-permute-start.10) | collective-permute-done | bytes 524320 | tf_op jit(solution)/shard_map/ppermute | solution.py:81
  197.6 6.9 %collective-permute-done.13 = bf16[1,2,256,128]{3,2,1,0:T(8,128)(2,1)S(1)} collective-permute-done((bf16[1,2,256,128]{3,2,1,0:T(8,128)(2,1)}, bf16[1,2,256,128]{3,2,1,0:T(8,128)(2,1)S(1)}, u32[]{:S(2)}, u32[]{:S(2)}) %collective-permute-start.13) | collective-permute-done | bytes 131104 | tf_op jit(solution)/shard_map/ppermute | solution.py:81
  206.6 16.6 %experts_forward.1 = (f32[8,256,512]{2,1,0:T(8,128)}, bf16[8,4,256,256]{3,2,1,0:T(8,128)(2,1)}, bf16[8,4,256,256]{3,2,1,0:T(8,128)(2,1)}) custom-call(bf16[256,512]{1,0:T(8,128)(2,1)} %copy.86.x_ref, bf16[8,4,2,8,64,256]{5,4,3,2,1,0:T(8,128)(2,1)} %bitcast.231), custom_call_target="tpu_custom_call" | custom-call | flops 17600000000 | bytes 48000000 | tf_op jit(solution)/shard_map/experts_forward/pallas_call | solution.py:770
  223.2 18.1 %towers.1 = (bf16[8,256,512]{2,1,0:T(8,128)(2,1)}, bf16[8,512,256]{2,1,0:T(8,128)(2,1)}, f32[256,512]{1,0:T(8,128)}, bf16[5,512,128]{2,1,0:T(8,128)(2,1)}, bf16[...) custom-call(bf16[256,512]{1,0:T(8,128)(2,1)} %copy.86.x_ref, f32[8,256,512]{2,1,0:T(8,128)} %get-tuple-element.106.y_ref, ...), custom_call_target="tpu_custom_call" | custom-call | flops 13200000000 | bytes 36000000 | tf_op jit(solution)/shard_map/towers/pallas_call | solution.py:786
  241.3 15.1 %experts_back_rows.1 = (bf16[8,4,256,256]{3,2,1,0:T(8,128)(2,1)}, bf16[256,128]{1,0:T(8,128)(2,1)}, bf16[256,128]{1,0:T(8,128)(2,1)}, bf16[256,128]{1,0:T(8,128)(2,1)}, bf16[256,128]{1,0:T(8,128)(2,1)}) custom-call(bf16[8,256,512]{2,1,0:T(8,128)(2,1)} %get-tuple-element.107.d_ref, bf16[8,4,2,8,64,256]{5,4,3,2,1,0:T(8,128)(2,1)} %bitcast.232, ...), custom_call_target="tpu_custom_call" | custom-call | flops 15399999488 | bytes 42000000 | tf_op jit(solution)/shard_map/experts_back_rows/pallas_call | solution.py:810
  263.4 9.6 %experts_back_out.1.refs_4_.refs_1_.refs_2_ = bf16[32,8,64,256]{3,2,1,0:T(8,128)(2,1)} custom-call(bf16[8,512,256]{2,1,0:T(8,128)(2,1)} %get-tuple-element.115.lhs_ref, bf16[8,4,256,256]{3,2,1,0:T(8,128)(2,1)} %get-tuple-element.116.rows_ref), custom_call_target="tpu_custom_call" | custom-call | flops 9900000256 | bytes 27000000 | tf_op jit(solution)/shard_map/experts_back_out/pallas_call | solution.py:870
  273.0 6.0 %collective-permute-done.16.refs_3_ = bf16[1,1056,128]{2,1,0:T(8,128)(2,1)S(1)} collective-permute-done((bf16[1,1056,128]{2,1,0:T(8,128)(2,1)S(1)}, bf16[1,1056,128]{2,1,0:T(8,128)(2,1)S(1)}, u32[]{:S(2)}, u32[]{:S(2)}) %collective-permute-start.16) | collective-permute-done | bytes 270368 | tf_op jit(solution)/shard_map/ppermute | solution.py:81
  285.3 8.8 %experts_back_in.1 = (bf16[16,8,64,256]{3,2,1,0:T(8,128)(2,1)}, bf16[16,8,64,256]{3,2,1,0:T(8,128)(2,1)}) custom-call(s32[1]{0:T(128)} %bitcast.me, bf16[1,512,256]{2,1,0:T(8,128)(2,1)} %bitcast.196, bf16[8,4,256,256]{3,2,1,0:T(8,128)(2,1)} %get-tuple-element.117.rows_ref, bf16[4,1056,128]{2,1,0:T(8,128)(2,1)} %join.4.refs_0_, ...), custom_call_target="tpu_custom_call" | custom-call | flops 9900000256 | bytes 27000000 | tf_op jit(solution)/shard_map/experts_back_in/pallas_call | solution.py:883
  296.6 5.2 collective-permute-done.21
  309.0 22.3 %collective-permute-done.22 = bf16[1,1536,128]{2,1,0:T(8,128)(2,1)S(1)} collective-permute-done((bf16[1,1536,128]{2,1,0:T(8,128)(2,1)}, bf16[1,1536,128]{2,1,0:T(8,128)(2,1)S(1)}, u32[]{:S(2)}, u32[]{:S(2)}) %collective-permute-start.22) | collective-permute-done | bytes 393248 | tf_op jit(solution)/shard_map/ppermute | solution.py:81
  334.0 7.6 %sum_core_w.1 = (bf16[32,64,256]{2,1,0:T(8,128)(2,1)}, bf16[32,64,256]{2,1,0:T(8,128)(2,1)}, bf16[32,64,256]{2,1,0:T(8,128)(2,1)}, bf16[32,64,256]{2,1,0:T(8,128)(2,1)}) custom-call(bf16[4,32,64,256]{3,2,1,0:T(8,128)(2,1)} %bitcast.182, bf16[4,32,64,256]{3,2,1,0:T(8,128)(2,1)} %bitcast.45.refs_1_, bf16[1,1536,128]{2,1,0:T(8,128)(2,1)} %sum_small.6.refs_2_), custom_call_target="tpu_custom_call" | custom-call | tf_op jit(solution)/shard_map/sum_core_w/pallas_call | solution.py:117
  351.7 11.2 %collective-permute-done.30 = bf16[1,1536,128]{2,1,0:T(8,128)(2,1)S(1)} collective-permute-done((bf16[1,1536,128]{2,1,0:T(8,128)(2,1)S(1)}, bf16[1,1536,128]{2,1,0:T(8,128)(2,1)S(1)}, u32[]{:S(2)}, u32[]{:S(2)}) %collective-permute-start.30) | collective-permute-done | bytes 393248 | tf_op jit(solution)/shard_map/ppermute | solution.py:81
  366.6 33.1 %scatter.4 = (f32[4,128,8192]{2,1,0:T(8,128)}, f32[4,128,8192]{2,1,0:T(8,128)}, f32[4,128,8192]{2,1,0:T(8,128)}) custom-call(s32[1]{0:T(128)} %bitcast.me, s32[256]{0:T(256)} %reshape_squeeze.3.bounds, s32[65536]{0:T(1024)} %bitcast.245, s32[512,128]{1,0:T(8,128)} %get-tuple-element.83.samples, bf16[16,288,128]{2,1,0:T(8,128)(2,1)} %join.5.refs_2_.own, ...), custom_call_target="tpu_custom_call" | custom-call | flops 28600000512 | bytes 78000000 | tf_op jit(solution)/shard_map/scatter/pallas_call | solution.py:836
  406.6 7.9 %collective-permute-done.32 = bf16[1,1536,128]{2,1,0:T(8,128)(2,1)S(1)} collective-permute-done((bf16[1,1536,128]{2,1,0:T(8,128)(2,1)S(1)}, bf16[1,1536,128]{2,1,0:T(8,128)(2,1)S(1)}, u32[]{:S(2)}, u32[]{:S(2)}) %collective-permute-start.32) | collective-permute-done | bytes 393248 | tf_op jit(solution)/shard_map/ppermute | solution.py:81
  418.1 34.1 %scatter.5 = (f32[4,128,8192]{2,1,0:T(8,128)}, f32[4,128,8192]{2,1,0:T(8,128)}, f32[4,128,8192]{2,1,0:T(8,128)}) custom-call(s32[1]{0:T(128)} %bitcast.me, s32[256]{0:T(256)} %reshape_squeeze.3.bounds, s32[65536]{0:T(1024)} %bitcast.246, s32[512,128]{1,0:T(8,128)} %get-tuple-element.83.samples, ...), custom_call_target="tpu_custom_call", output_to_operand_aliasing={{0}: (9, {}), {1}: (10, {}), {2}: (11, {})} | custom-call | flops 28600000512 | bytes 78000000 | tf_op jit(solution)/shard_map/scatter/pallas_call | solution.py:836
  474.7 34.5 %scatter.6 = (f32[4,128,8192]{2,1,0:T(8,128)}, f32[4,128,8192]{2,1,0:T(8,128)}, f32[4,128,8192]{2,1,0:T(8,128)}) custom-call(s32[1]{0:T(128)} %bitcast.me, s32[256]{0:T(256)} %reshape_squeeze.3.bounds, s32[65536]{0:T(1024)} %bitcast.247, s32[512,128]{1,0:T(8,128)} %get-tuple-element.83.samples, ...), custom_call_target="tpu_custom_call", output_to_operand_aliasing={{0}: (9, {}), {1}: (10, {}), {2}: (11, {})} | custom-call | flops 28600000512 | bytes 78000000 | tf_op jit(solution)/shard_map/scatter/pallas_call | solution.py:836
  517.3 33.8 %scatter.7 = (f32[4,128,8192]{2,1,0:T(8,128)}, f32[4,128,8192]{2,1,0:T(8,128)}, f32[4,128,8192]{2,1,0:T(8,128)}) custom-call(s32[1]{0:T(128)} %bitcast.me, s32[256]{0:T(256)} %reshape_squeeze.3.bounds, s32[65536]{0:T(1024)} %bitcast.248, s32[512,128]{1,0:T(8,128)} %get-tuple-element.83.samples, ...), custom_call_target="tpu_custom_call", output_to_operand_aliasing={{0}: (9, {}), {1}: (10, {}), {2}: (11, {})} | custom-call | flops 28600000512 | bytes 78000000 | tf_op jit(solution)/shard_map/scatter/pallas_call | solution.py:836
  (264 shorter events, 141.6 us)
Async XLA Ops:
  7.2 199.4 %all-gather.2.cloned.1.call-start = ((), (), s32[]{:S(2)}) async-start(), calls=%async_computation.2 | async-start | bytes 17301504 | tf_op jit(solution)/shard_map/all_gather | solution.py:667
  36.3 516.3 %reduce-scatter.2.cloned.1.call-start = ((), (), s32[]{:S(2)}) async-start(), calls=%async_computation.3 | async-start | bytes 8650752 | tf_op jit(solution)/shard_map/reduce_scatter | solution.py:882
  123.3 24.2 %collective-permute-start.2 = (bf16[4,2,256,128]{3,2,1,0:T(8,128)(2,1)}, bf16[4,2,256,128]{3,2,1,0:T(8,128)(2,1)S(1)}, u32[]{:S(2)}, u32[]{:S(2)}) collective-permute-start(bf16[4,2,256,128]{3,2,1,0:T(8,128)(2,1)} %bitcast.240), channel_id=1, source_target_pairs={{0,4},{1,5},{2,6},{3,7},{4,0},{5,1},{6,2},{7,3},{8,12},{9,13},{10,... | collective-permute-start | bytes 1572872 | tf_op jit(solution)/shard_map/ppermute | solution.py:81
  160.8 26.5 %collective-permute-start.10 = (bf16[4,2,256,128]{3,2,1,0:T(8,128)(2,1)}, bf16[4,2,256,128]{3,2,1,0:T(8,128)(2,1)S(1)}, u32[]{:S(2)}, u32[]{:S(2)}) collective-permute-start(bf16[4,2,256,128]{3,2,1,0:T(8,128)(2,1)} %bitcast.236), channel_id=1, source_target_pairs={{0,6},{1,7},{2,4},{3,5},{4,2},{5,3},{6,0},{7,1},{8,14},{9,15},{10,... | collective-permute-start | bytes 1572872 | tf_op jit(solution)/shard_map/ppermute | solution.py:81
  165.0 25.6 %collective-permute-start.5 = (bf16[1,2,256,128]{3,2,1,0:T(8,128)(2,1)}, bf16[1,2,256,128]{3,2,1,0:T(8,128)(2,1)}, u32[]{:S(2)}, u32[]{:S(2)}) collective-permute-start(bf16[1,2,256,128]{3,2,1,0:T(8,128)(2,1)} %bitcast.17), channel_id=1, source_target_pairs={{0,16},{1,17},{2,18},{3,19},{4,20},{5,21},{6,22},{7,23},{8,24},{9,... | collective-permute-start | bytes 393224 | tf_op jit(solution)/shard_map/ppermute | solution.py:81
  165.0 29.0 %collective-permute-start.4 = (bf16[1,2,256,128]{3,2,1,0:T(8,128)(2,1)}, bf16[1,2,256,128]{3,2,1,0:T(8,128)(2,1)}, u32[]{:S(2)}, u32[]{:S(2)}) collective-permute-start(bf16[1,2,256,128]{3,2,1,0:T(8,128)(2,1)} %bitcast.16), channel_id=1, source_target_pairs={{0,8},{1,9},{2,10},{3,11},{4,12},{5,13},{6,14},{7,15},{8,0},{9,1},... | collective-permute-start | bytes 393224 | tf_op jit(solution)/shard_map/ppermute | solution.py:81
  294.1 39.9 %collective-permute-start.20 = (bf16[16,8,64,256]{3,2,1,0:T(8,128)(2,1)}, bf16[16,8,64,256]{3,2,1,0:T(8,128)(2,1)}, u32[]{:S(2)}, u32[]{:S(2)}) collective-permute-start(bf16[16,8,64,256]{3,2,1,0:T(8,128)(2,1)} %get-tuple-element.119), channel_id=1, source_target_pairs={{0,1},{1,0},{2,3},{3,2},{4,5},{5,4},{6,7},{7,6},{8,9},{9,8},{10,11... | collective-permute-start | bytes 12582920 | tf_op jit(solution)/shard_map/ppermute | solution.py:81
  304.6 26.7 %collective-permute-start.22 = (bf16[1,1536,128]{2,1,0:T(8,128)(2,1)}, bf16[1,1536,128]{2,1,0:T(8,128)(2,1)S(1)}, u32[]{:S(2)}, u32[]{:S(2)}) collective-permute-start(bf16[1,1536,128]{2,1,0:T(8,128)(2,1)} %sum_small.5), channel_id=1, source_target_pairs={{0,2},{1,3},{2,0},{3,1},{4,6},{5,7},{6,4},{7,5},{8,10},{9,11},{10,... | collective-permute-start | bytes 1179656 | tf_op jit(solution)/shard_map/ppermute | solution.py:81
  305.4 36.2 %collective-permute-start.19 = (bf16[4,288,128]{2,1,0:T(8,128)(2,1)S(1)}, bf16[4,288,128]{2,1,0:T(8,128)(2,1)S(1)}, u32[]{:S(2)}, u32[]{:S(2)}) collective-permute-start(bf16[4,288,128]{2,1,0:T(8,128)(2,1)S(1)} %slice.46.refs_0_), channel_id=1, source_target_pairs={{0,6},{1,7},{2,4},{3,5},{4,2},{5,3},{6,0},{7,1},{8,14},{9,15},{10,... | collective-permute-start | bytes 884744 | tf_op jit(solution)/shard_map/ppermute | solution.py:81
  306.8 34.8 %collective-permute-start.18 = (bf16[4,288,128]{2,1,0:T(8,128)(2,1)S(1)}, bf16[4,288,128]{2,1,0:T(8,128)(2,1)S(1)}, u32[]{:S(2)}, u32[]{:S(2)}) collective-permute-start(bf16[4,288,128]{2,1,0:T(8,128)(2,1)S(1)} %slice.46.refs_0_), channel_id=1, source_target_pairs={{0,4},{1,5},{2,6},{3,7},{4,0},{5,1},{6,2},{7,3},{8,12},{9,13},{10,... | collective-permute-start | bytes 884744 | tf_op jit(solution)/shard_map/ppermute | solution.py:81
  308.2 35.1 %collective-permute-start.17 = (bf16[4,288,128]{2,1,0:T(8,128)(2,1)S(1)}, bf16[4,288,128]{2,1,0:T(8,128)(2,1)S(1)}, u32[]{:S(2)}, u32[]{:S(2)}) collective-permute-start(bf16[4,288,128]{2,1,0:T(8,128)(2,1)S(1)} %slice.46.refs_0_), channel_id=1, source_target_pairs={{0,2},{1,3},{2,0},{3,1},{4,6},{5,7},{6,4},{7,5},{8,10},{9,11},{10,... | collective-permute-start | bytes 884744 | tf_op jit(solution)/shard_map/ppermute | solution.py:81
  348.2 51.6 %collective-permute-start.29 = (bf16[4,256,128]{2,1,0:T(8,128)(2,1)S(1)}, bf16[4,256,128]{2,1,0:T(8,128)(2,1)S(1)}, u32[]{:S(2)}, u32[]{:S(2)}) collective-permute-start(bf16[4,256,128]{2,1,0:T(8,128)(2,1)S(1)} %slice.50.refs_0_), channel_id=1, source_target_pairs={{0,6},{1,7},{2,4},{3,5},{4,2},{5,3},{6,0},{7,1},{8,14},{9,15},{10,... | collective-permute-start | bytes 786440 | tf_op jit(solution)/shard_map/ppermute | solution.py:81
  350.6 49.2 %collective-permute-start.28 = (bf16[4,256,128]{2,1,0:T(8,128)(2,1)S(1)}, bf16[4,256,128]{2,1,0:T(8,128)(2,1)S(1)}, u32[]{:S(2)}, u32[]{:S(2)}) collective-permute-start(bf16[4,256,128]{2,1,0:T(8,128)(2,1)S(1)} %slice.50.refs_0_), channel_id=1, source_target_pairs={{0,4},{1,5},{2,6},{3,7},{4,0},{5,1},{6,2},{7,3},{8,12},{9,13},{10,... | collective-permute-start | bytes 786440 | tf_op jit(solution)/shard_map/ppermute | solution.py:81
  350.8 49.0 %collective-permute-start.27 = (bf16[4,256,128]{2,1,0:T(8,128)(2,1)S(1)}, bf16[4,256,128]{2,1,0:T(8,128)(2,1)S(1)}, u32[]{:S(2)}, u32[]{:S(2)}) collective-permute-start(bf16[4,256,128]{2,1,0:T(8,128)(2,1)S(1)} %slice.50.refs_0_), channel_id=1, source_target_pairs={{0,2},{1,3},{2,0},{3,1},{4,6},{5,7},{6,4},{7,5},{8,10},{9,11},{10,... | collective-permute-start | bytes 786440 | tf_op jit(solution)/shard_map/ppermute | solution.py:81
  403.0 49.2 %collective-permute-start.26 = (bf16[4,512,128]{2,1,0:T(8,128)(2,1)S(1)}, bf16[4,512,128]{2,1,0:T(8,128)(2,1)S(1)}, u32[]{:S(2)}, u32[]{:S(2)}) collective-permute-start(bf16[4,512,128]{2,1,0:T(8,128)(2,1)S(1)} %slice.49.refs_0_), channel_id=1, source_target_pairs={{0,6},{1,7},{2,4},{3,5},{4,2},{5,3},{6,0},{7,1},{8,14},{9,15},{10,... | collective-permute-start | bytes 1572872 | tf_op jit(solution)/shard_map/ppermute | solution.py:81
  403.1 49.2 %collective-permute-start.25 = (bf16[4,512,128]{2,1,0:T(8,128)(2,1)S(1)}, bf16[4,512,128]{2,1,0:T(8,128)(2,1)S(1)}, u32[]{:S(2)}, u32[]{:S(2)}) collective-permute-start(bf16[4,512,128]{2,1,0:T(8,128)(2,1)S(1)} %slice.49.refs_0_), channel_id=1, source_target_pairs={{0,4},{1,5},{2,6},{3,7},{4,0},{5,1},{6,2},{7,3},{8,12},{9,13},{10,... | collective-permute-start | bytes 1572872 | tf_op jit(solution)/shard_map/ppermute | solution.py:81
  403.2 49.1 %collective-permute-start.24 = (bf16[4,512,128]{2,1,0:T(8,128)(2,1)S(1)}, bf16[4,512,128]{2,1,0:T(8,128)(2,1)S(1)}, u32[]{:S(2)}, u32[]{:S(2)}) collective-permute-start(bf16[4,512,128]{2,1,0:T(8,128)(2,1)S(1)} %slice.49.refs_0_), channel_id=1, source_target_pairs={{0,2},{1,3},{2,0},{3,1},{4,6},{5,7},{6,4},{7,5},{8,10},{9,11},{10,... | collective-permute-start | bytes 1572872 | tf_op jit(solution)/shard_map/ppermute | solution.py:81
  417.2 39.2 %collective-permute-start.34 = (bf16[1,1536,128]{2,1,0:T(8,128)(2,1)}, bf16[1,1536,128]{2,1,0:T(8,128)(2,1)S(1)}, u32[]{:S(2)}, u32[]{:S(2)}) collective-permute-start(bf16[1,1536,128]{2,1,0:T(8,128)(2,1)} %sum_small.8.refs_3_), channel_id=1, source_target_pairs={{0,16},{1,17},{2,18},{3,19},{4,20},{5,21},{6,22},{7,23},{8,24},{9,... | collective-permute-start | bytes 1179656 | tf_op jit(solution)/shard_map/ppermute | solution.py:81
  460.2 49.1 %collective-permute-start.35 = (bf16[4,8,64,256]{3,2,1,0:T(8,128)(2,1)}, bf16[4,8,64,256]{3,2,1,0:T(8,128)(2,1)}, u32[]{:S(2)}, u32[]{:S(2)}) collective-permute-start(bf16[4,8,64,256]{3,2,1,0:T(8,128)(2,1)} %bitcast.235), channel_id=1, source_target_pairs={{0,2},{1,3},{2,0},{3,1},{4,6},{5,7},{6,4},{7,5},{8,10},{9,11},{10,... | collective-permute-start | bytes 3145736 | tf_op jit(solution)/shard_map/ppermute | solution.py:81
  460.3 49.0 %collective-permute-start.36 = (bf16[4,8,64,256]{3,2,1,0:T(8,128)(2,1)}, bf16[4,8,64,256]{3,2,1,0:T(8,128)(2,1)}, u32[]{:S(2)}, u32[]{:S(2)}) collective-permute-start(bf16[4,8,64,256]{3,2,1,0:T(8,128)(2,1)} %bitcast.234), channel_id=1, source_target_pairs={{0,4},{1,5},{2,6},{3,7},{4,0},{5,1},{6,2},{7,3},{8,12},{9,13},{10,... | collective-permute-start | bytes 3145736 | tf_op jit(solution)/shard_map/ppermute | solution.py:81
  460.3 49.5 %collective-permute-start.37 = (bf16[4,8,64,256]{3,2,1,0:T(8,128)(2,1)}, bf16[4,8,64,256]{3,2,1,0:T(8,128)(2,1)}, u32[]{:S(2)}, u32[]{:S(2)}) collective-permute-start(bf16[4,8,64,256]{3,2,1,0:T(8,128)(2,1)} %bitcast.233), channel_id=1, source_target_pairs={{0,6},{1,7},{2,4},{3,5},{4,2},{5,3},{6,0},{7,1},{8,14},{9,15},{10,... | collective-permute-start | bytes 3145736 | tf_op jit(solution)/shard_map/ppermute | solution.py:81
  513.8 37.4 %collective-permute-start.39 = (bf16[1,8,64,256]{3,2,1,0:T(8,128)(2,1)}, bf16[1,8,64,256]{3,2,1,0:T(8,128)(2,1)S(1)}, u32[]{:S(2)}, u32[]{:S(2)}) collective-permute-start(bf16[1,8,64,256]{3,2,1,0:T(8,128)(2,1)} %bitcast.251), channel_id=1, source_target_pairs={{0,16},{1,17},{2,18},{3,19},{4,20},{5,21},{6,22},{7,23},{8,24},{9,... | collective-permute-start | bytes 786440 | tf_op jit(solution)/shard_map/ppermute | solution.py:81
  513.8 37.4 %collective-permute-start.38 = (bf16[1,8,64,256]{3,2,1,0:T(8,128)(2,1)}, bf16[1,8,64,256]{3,2,1,0:T(8,128)(2,1)S(1)}, u32[]{:S(2)}, u32[]{:S(2)}) collective-permute-start(bf16[1,8,64,256]{3,2,1,0:T(8,128)(2,1)} %bitcast.250), channel_id=1, source_target_pairs={{0,8},{1,9},{2,10},{3,11},{4,12},{5,13},{6,14},{7,15},{8,0},{9,1},... | collective-permute-start | bytes 786440 | tf_op jit(solution)/shard_map/ppermute | solution.py:81
  513.9 37.3 %collective-permute-start.40 = (bf16[1,8,64,256]{3,2,1,0:T(8,128)(2,1)}, bf16[1,8,64,256]{3,2,1,0:T(8,128)(2,1)S(1)}, u32[]{:S(2)}, u32[]{:S(2)}) collective-permute-start(bf16[1,8,64,256]{3,2,1,0:T(8,128)(2,1)} %bitcast.249), channel_id=1, source_target_pairs={{0,24},{1,25},{2,26},{3,27},{4,28},{5,29},{6,30},{7,31},{8,16},{9,... | collective-permute-start | bytes 786440 | tf_op jit(solution)/shard_map/ppermute | solution.py:81
  (76 other events, 781.4 us)
Sparse Core Ops, SparseCore 0:
  11.5 116.8 all-gather.1
  294.3 167.2 reduce-scatter.1
